TPU v7x, 32 devices: a whole 2x2x4 slice. The times are simulated.
32 devices in a mesh: batch: 2 (over x), head: 2 (over y), blk: 8 (over z, core).
Axes of the slice: x: 2, y: 2, z: 4, core: 2. Of those that a mesh axis runs over, the one named last changes fastest.
Arguments:
- tokens: bfloat16 [16, 2048, 1024], P(('batch', 'blk'), 'head'), parts along dimension 0, may hold values from -10.5 to 10.5
- proj_weight: bfloat16 [1024, 3072], replicated, may hold values from -0.1875 to 0.1875
- out_weight: bfloat16 [1024, 1024], replicated, may hold values from -1.5 to 1.5
- pattern: int32 [256, 16], P(('batch', 'blk')), parts along dimension 0, may hold values from 0 to 127, as said below
Outputs:
- mixed_out: bfloat16 [16, 2048, 1024], P(('batch', 'blk'), 'head'), parts along dimension 0
There are 2 independent parts, one for each index of `batch`. A program takes and returns all parts, laid end to end along the dimension named above; an argument that names none is the same for every part. Nothing has to cross between parts.
Inputs may be any that keep to these rules, and one draw needn't show every extreme that they name: `pattern`: row i lists first 6 distinct blocks j with |j - i| <= 8, among them i itself, then 10 distinct summary blocks j (j % 16 >= 12) with |j - i| > 8. Every row with 8 <= i < 120 lists i - 8 and i + 8.
All inputs are finite; a program needn't handle non-finite values.
Results may differ from a plain program's by a relative error of at most 0.0095.
Values may be sent and summed in bfloat16 or wider, within the bound.
No kernel may reach another device: no remote copies, remote signals or barrier semaphores. Data moves between devices by JAX's collectives and lax.ppermute only.
A program may use at most 128 MiB of HBM per device.

v0:
```python
import functools

import jax
import jax.numpy as jnp
from jax import lax
from jax.experimental import pallas as pl
from jax.experimental.pallas import tpu as pltpu
from jax.sharding import PartitionSpec as P

D = 1024
H = 16
HD = 64
BLK = 128
REACH = 8
LSEL = 6
SUMB = 4
SB = 16
KSEL = 16
PAIRS = H // 2
LANES = 2 * HD
TOTAL_CAP = 2.0**100


def split_kernel(weight_ref, query_ref, key_ref, value_ref):
    both = weight_ref[...]
    first, second = both[:, : 3 * HD], both[:, 3 * HD :]

    def columns(which):
        lo = which * HD
        return jnp.concatenate([first[:, lo : lo + HD], second[:, lo : lo + HD]], axis=1)

    query_ref[...] = columns(0).T
    key_ref[...] = columns(1)
    value_ref[...] = columns(2).T


def split_weights(proj_weight):
    wide = jax.ShapeDtypeStruct((D, D), jnp.bfloat16)
    across = pl.BlockSpec((LANES, D), lambda p: (p, 0))
    down = pl.BlockSpec((D, LANES), lambda p: (0, p))
    return pl.pallas_call(
        split_kernel,
        grid=(PAIRS,),
        in_specs=[pl.BlockSpec((D, 3 * LANES), lambda p: (0, p))],
        out_specs=[across, down, across],
        out_shape=[wide, wide, wide],
        cost_estimate=pl.CostEstimate(flops=0, bytes_accessed=4 * D * 3 * D, transcendentals=0),
        name="split_weights",
    )(proj_weight)


def attend_kernel(first, last, blocks, count, together, chunk, pieces, *refs):
    f32, bf16 = jnp.float32, jnp.bfloat16
    refs = list(refs)
    table_ref, query_ref = refs[:2]
    key_refs = refs[2 : 2 + pieces]
    value_refs = refs[2 + pieces : 2 + 2 * pieces]
    refs = refs[2 + 2 * pieces :]
    if not first:
        sum_in_ref, row_in_ref = refs[:2]
        refs = refs[2:]
    if last:
        out_ref = refs.pop(0)
    else:
        sum_out_ref, row_out_ref = refs[:2]
        refs = refs[2:]
    if pieces == 1:
        key_ref, value_ref = key_refs[0], value_refs[0]
    else:
        key_ref, value_ref = refs
        start = 0
        for key_piece, value_piece in zip(key_refs, value_refs):
            size = key_piece.shape[0]
            key_ref[start : start + size, :] = key_piece[...]
            value_ref[:, start : start + size] = value_piece[...]
            start += size

    row = lax.broadcasted_iota(jnp.int32, (LANES, BLK), 0)

    def at(index, size=BLK):
        return pl.ds(pl.multiple_of(index * size, size), size)

    def queries(index):
        own = query_ref[:, at(index)]
        zero = jnp.zeros_like(own)
        return jnp.concatenate([jnp.where(row < HD, own, zero), jnp.where(row < HD, zero, own)], axis=1)

    def places(index, which):
        return [pl.multiple_of(table_ref[index, which + n] * BLK, BLK) for n in range(chunk)]

    def score(index, which, query):
        keys = [key_ref[pl.ds(place, BLK), :] for place in places(index, which)]
        return jnp.dot(jnp.concatenate(keys, axis=0), query, preferred_element_type=f32)

    def values(index, which):
        return jnp.concatenate([value_ref[:, pl.ds(place, BLK)] for place in places(index, which)], axis=1)

    def gather(picked, raised):
        ones = jnp.ones((16, raised.shape[0]), bf16)
        return jnp.dot(jnp.concatenate([picked, ones], axis=0), raised, preferred_element_type=f32)

    def by_head(rows):
        return jnp.where(row < HD, rows[:, :BLK], rows[:, BLK:])

    def finish(index, shift, total, rescale=None):
        mine = jnp.concatenate([total[:HD, :BLK], total[HD:LANES, BLK:]], axis=0)
        count_all = total[LANES : LANES + 1]
        if not first:
            before = sum_in_ref[:, at(index)]
            count_before = row_in_ref[0, 1:2, at(index, 2 * BLK)]
            if rescale is not None:
                before = before * by_head(rescale)
                count_before = count_before * rescale
            mine = mine + before
            count_all = count_all + count_before
        if last:
            out_ref[at(index), :] = (mine * by_head(1.0 / count_all)).T.astype(bf16)
        else:
            sum_out_ref[:, at(index)] = mine
            row_out_ref[0, 0:1, at(index, 2 * BLK)] = shift
            row_out_ref[0, 1:2, at(index, 2 * BLK)] = count_all
        return count_all

    def one(index):
        query = queries(index)
        total = None
        shift = None if first else row_in_ref[0, 0:1, at(index, 2 * BLK)]
        for which in range(0, count, chunk):
            scores = score(index, which, query)
            if shift is None:
                shift = jnp.max(scores, axis=0, keepdims=True)
            part = gather(values(index, which), jnp.exp(scores - shift).astype(bf16))
            total = part if total is None else total + part
        return finish(index, shift, total)

    def whole_row(index):
        query = queries(index)
        shift = jnp.full((1, 2 * BLK), -jnp.inf, f32) if first else row_in_ref[0, 0:1, at(index, 2 * BLK)]
        old = shift

        def largest(n, shift):
            return jnp.maximum(shift, jnp.max(score(index, chunk * n, query), axis=0, keepdims=True))

        shift = lax.fori_loop(0, count // chunk, largest, shift)

        def add(n, total):
            raised = jnp.exp(score(index, chunk * n, query) - shift).astype(bf16)
            return total + gather(values(index, chunk * n), raised)

        total = lax.fori_loop(0, count // chunk, add, jnp.zeros((LANES + 16, 2 * BLK), f32))
        finish(index, shift, total, None if first else jnp.exp(old - shift))

    def body(number, peak):
        for n in range(together):
            peak = jnp.maximum(peak, one(number * together + n))
        return peak

    peak = lax.fori_loop(0, blocks // together, body, jnp.zeros((1, 2 * BLK), f32))

    @pl.when(jnp.logical_not(jnp.max(peak) <= TOTAL_CAP))
    def _():
        lax.fori_loop(0, blocks, lambda index, carry: (whole_row(index), carry)[1], 0)


def attend(name, table, query, keys, values, state, last, together, chunk):
    f32, bf16 = jnp.float32, jnp.bfloat16
    rows = query.shape[1]
    blocks = rows // BLK
    count = table.shape[1]
    while blocks % together:
        together //= 2
    total_rows = sum(key.shape[0] for key in keys)
    across = lambda array: pl.BlockSpec((LANES, array.shape[1]), lambda p: (p, 0))
    down = lambda array: pl.BlockSpec((array.shape[0], LANES), lambda p: (0, p))
    per_row = pl.BlockSpec((1, 2, 2 * rows), lambda p: (p, 0, 0))
    in_specs = [pl.BlockSpec(memory_space=pltpu.SMEM), across(query)]
    in_specs += [down(key) for key in keys] + [across(value) for value in values]
    if state:
        in_specs += [across(query), per_row]
    if last:
        out_specs = pl.BlockSpec((rows, LANES), lambda p: (0, p))
        out_shape = jax.ShapeDtypeStruct((rows, D), bf16)
    else:
        out_specs = [across(query), per_row]
        out_shape = [jax.ShapeDtypeStruct((D, rows), f32), jax.ShapeDtypeStruct((PAIRS, 2, 2 * rows), f32)]
    scratch = [pltpu.VMEM((total_rows, LANES), bf16), pltpu.VMEM((LANES, total_rows), bf16)]
    scores = rows * count * BLK * H
    return pl.pallas_call(
        functools.partial(attend_kernel, not state, last, blocks, count, together, chunk, len(keys)),
        grid=(PAIRS,),
        in_specs=in_specs,
        out_specs=out_specs,
        out_shape=out_shape,
        scratch_shapes=scratch if len(keys) > 1 else [],
        compiler_params=pltpu.CompilerParams(vmem_limit_bytes=18 * 2**20),
        cost_estimate=pl.CostEstimate(
            flops=24 * scores * HD, bytes_accessed=4 * total_rows * D + 10 * rows * D, transcendentals=scores
        ),
        name=name,
    )(table, query, *keys, *values, *state)


def project_rows(rows, weight):
    return jnp.dot(rows, weight, preferred_element_type=jnp.float32).astype(jnp.bfloat16)


def project_columns(weight, rows, scale=1.0):
    wide = lax.dot_general(weight, rows, (((1,), (1,)), ((), ())), preferred_element_type=jnp.float32)
    return (wide * scale).astype(jnp.bfloat16)


def rows_by_axes(own, weights, place, stride, strides):
    summary = SUMB * BLK
    half = summary // 2
    cut = own.shape[0] - summary
    chips = strides // 2
    low = place == 0
    swap = lambda rows: lax.ppermute(rows, "head", [(0, 1), (1, 0)])
    beside = lambda rows: lax.ppermute(rows, "blk", [(s, s ^ 1) for s in range(strides)])

    def along(rows, k):
        return lax.ppermute(rows, "blk", [(s, (s + 2 * k) % strides) for s in range(strides)])

    steps = []
    for s in range(strides - 1):
        steps += [(s, s + 1), (strides + s + 1, strides + s)]
    to_next = lambda rows: lax.ppermute(rows, ("head", "blk"), steps)

    other_mid = swap(own[cut : cut + half])
    other_mid, own, weights = lax.optimization_barrier((other_mid, own, weights))
    carried = jnp.where(low, other_mid, own[cut + half :])
    other_low, other_top = swap(own[:cut]), swap(own[cut + half :])
    slots = [None] * chips
    slots[2:-1] = [along(carried, k) for k in range(2, chips - 1)]
    slots[1] = along(carried, 1)
    slots[1], carried = lax.optimization_barrier((slots[1], carried))
    slots[-1] = along(carried, chips - 1)
    slots = [jnp.concatenate([rows, swap(rows)], axis=0) for rows in slots[1:]]
    other_high = jnp.concatenate([other_mid, other_top], axis=0)
    edge_low = to_next(other_low)
    edge_high = to_next(other_high)
    pieces = [own, other_low, other_high, edge_low, edge_high, beside(jnp.where(low, other_high, own[cut:]))]
    for rows in slots:
        pieces += [rows, beside(rows)]

    def position(block):
        of, inside = block // SB, block % SB
        rel = block - stride * SB
        mine = inside % 8 + jnp.where(inside // 8 == place, 0, 8)
        edge = jnp.where(rel < 0, rel + SB + 8, rel)
        order = inside - (SB - SUMB)
        k = (stride // 2 - of // 2) % chips
        turned = (order // 2 ^ place) * 2 + order % 2
        far = 28 + (k - 1) * 8 + jnp.where(of % 2 == stride % 2, 0, 4) + turned
        far = jnp.where(k == 0, 24 + order, far)
        return jnp.where(of == stride, mine, edge), jnp.where(of == stride, mine, far)

    return pieces, weights, position


def rows_by_gather(own, place, stride, strides, heads):
    summary = SUMB * BLK
    share = summary // heads
    lower = place < heads // 2
    stride_rows = lax.all_gather(own, "head", axis=0, tiled=True)
    piece = lax.dynamic_slice_in_dim(stride_rows[-summary:], place * share, share, 0)
    far_rows = lax.all_gather(piece, ("blk", "head"), axis=0, tiled=True)
    half = stride_rows.shape[0] // 2
    steps = []
    for h in range(heads):
        for s in range(strides - 1):
            ends = (h * strides + s, h * strides + s + 1)
            steps.append(ends if h < heads // 2 else ends[::-1])
    edge = lax.ppermute(jnp.where(lower, stride_rows[half:], stride_rows[:half]), ("head", "blk"), steps)

    def position(block):
        rel = block - stride * SB
        near = jnp.where(rel < 0, rel + SB + REACH, rel)
        return near, SB + REACH + block // SB * SUMB + block % SB - (SB - SUMB)

    return [stride_rows, edge, far_rows], position


def on_device(tokens, proj_weight, out_weight, pattern):
    heads = lax.axis_size("head")
    strides = lax.axis_size("blk")
    place = lax.axis_index("head")
    stride = lax.axis_index("blk")
    own = tokens[0]
    blocks = own.shape[0] // BLK
    weights = split_weights(proj_weight)

    if heads == 2:
        pieces, weights, position = rows_by_axes(own, weights, place, stride, strides)
        own = pieces[0]
    else:
        pieces, position = rows_by_gather(own, place, stride, strides, heads)
    listed = lax.dynamic_slice_in_dim(pattern, place * blocks, blocks, 0)
    near, far = position(listed)
    column = lax.broadcasted_iota(jnp.int32, listed.shape, 1)
    table = jnp.where(column < LSEL, near, far)

    query_weight, key_weight, value_weight = weights
    query = project_columns(query_weight, own, HD**-0.5)
    keys = [project_rows(rows, key_weight) for rows in pieces]
    values = [project_columns(value_weight, rows) for rows in pieces]
    mixed = attend("attend", table, query, keys, values, [], True, 2, 4)
    out = jnp.dot(mixed, out_weight, preferred_element_type=jnp.float32).astype(jnp.bfloat16)
    return out.reshape(tokens.shape)


def solution(mesh):
    return jax.shard_map(
        on_device,
        mesh=mesh,
        in_specs=(P(("batch", "blk"), "head", None), P(), P(), P(("batch", "blk"), None)),
        out_specs=P(("batch", "blk"), "head", None),
        check_vma=False,
    )
```

profile of v0, /device:TPU:11, one launch (start us, length us, event | category | flops | bytes accessed | tf_op | source)
XLA Modules:
  0.0 186.7 jit_solution(1282516416394582170)
XLA Ops:
  1.2 1.3 collective-permute-start
  2.5 8.6 %split_weights.1 = (bf16[1024,1024]{1,0:T(8,128)(2,1)}, bf16[1024,1024]{1,0:T(8,128)(2,1)}, bf16[1024,1024]{1,0:T(8,128)(2,1)}) custom-call(bf16[1024,3072]{1,0:T(8,128)(2,1)} %weight_ref.1), custom_call_target="tpu_custom_call" | custom-call | bytes 12582912 | tf_op jit(solution)/shard_map/split_weights/pallas_call | solution.py:41
  11.2 2.9 %collective-permute-done = bf16[256,1024]{1,0:T(8,128)(2,1)S(1)} collective-permute-done((bf16[256,1024]{1,0:T(8,128)(2,1)S(1)}, bf16[256,1024]{1,0:T(8,128)(2,1)S(1)}, u32[]{:S(2)}, u32[]{:S(2)}) %collective-permute-start) | collective-permute-done | bytes 524320 | tf_op jit(solution)/shard_map/ppermute | solution.py:218
  14.1 1.3 broadcast_select_fusion
  15.4 1.3 collective-permute-start.6
  19.1 4.0 %convolution_convert_fusion.refs_14_ = bf16[1024,1024]{1,0:T(8,128)(2,1)S(1)} fusion(bf16[1024,1024]{1,0:T(8,128)(2,1)} %get-tuple-element.24, bf16[1024,1024]{1,0:T(8,128)(2,1)S(1)} %bitcast.58), kind=kOutput, calls=%fused_computation.2 | convolution fusion | flops 2148532224 | bytes 6291456 | tf_op jit(solution)/shard_map/dot_general | solution.py:208
  23.1 2.3 %convolution_convert_fusion.1.refs_2_ = bf16[1024,1024]{1,0:T(8,128)(2,1)S(1)} fusion(bf16[1024,1024]{1,0:T(8,128)(2,1)S(1)} %bitcast.59, bf16[1024,1024]{1,0:T(8,128)(2,1)S(1)} %copy-done.3), kind=kOutput, calls=%fused_computation.3 | convolution fusion | flops 2148532224 | bytes 6291456 | tf_op jit(solution)/shard_map/dot_general | solution.py:204
  25.5 2.4 %multiply_convert_fusion.refs_1_ = bf16[1024,1024]{1,0:T(8,128)(2,1)S(1)} fusion(bf16[1024,1024]{1,0:T(8,128)(2,1)S(1)} %copy-done.5, bf16[1024,1024]{1,0:T(8,128)(2,1)S(1)} %bitcast.60), kind=kOutput, calls=%fused_computation | convolution fusion | flops 2149580800 | bytes 6291456 | tf_op jit(solution)/shard_map/dot_general | solution.py:208
  27.9 1.5 collective-permute-done.2
  29.6 5.1 %collective-permute-start.4 = (bf16[512,1024]{1,0:T(8,128)(2,1)S(1)}, bf16[512,1024]{1,0:T(8,128)(2,1)S(1)}, u32[]{:S(2)}, u32[]{:S(2)}) collective-permute-start(bf16[512,1024]{1,0:T(8,128)(2,1)S(1)} %constant_dynamic-update-slice_fusion), channel_id=1, source_target_pairs={{0,1},{9,8},{1,2},{10,9},{2,3},{11,10},{3,4},{12,11},{4,5},{13,12}... | collective-permute-start | bytes 3145736 | tf_op jit(solution)/shard_map/ppermute | solution.py:227
  35.8 1.3 convolution_convert_fusion.11.refs_16_
  37.1 1.6 collective-permute-start.12
  39.0 15.6 %collective-permute-done.9 = bf16[256,1024]{1,0:T(8,128)(2,1)S(1)} collective-permute-done((bf16[256,1024]{1,0:T(8,128)(2,1)S(1)}, bf16[256,1024]{1,0:T(8,128)(2,1)S(1)}, u32[]{:S(2)}, u32[]{:S(2)}) %collective-permute-start.9) | collective-permute-done | bytes 524320 | tf_op jit(solution)/shard_map/ppermute | solution.py:222
  54.5 10.2 %collective-permute-start.5 = (bf16[512,1024]{1,0:T(8,128)(2,1)S(1)}, bf16[512,1024]{1,0:T(8,128)(2,1)S(1)}, u32[]{:S(2)}, u32[]{:S(2)}) collective-permute-start(bf16[512,1024]{1,0:T(8,128)(2,1)S(1)} %get-tuple-element.27), channel_id=1, source_target_pairs={{0,1},{1,0},{2,3},{3,2},{4,5},{5,4},{6,7},{7,6},{8,9},{9,8},{10,11... | collective-permute-start | bytes 3145736 | tf_op jit(solution)/shard_map/ppermute | solution.py:219
  66.1 1.3 convolution_convert_fusion.7.refs_20_
  68.8 11.3 %collective-permute-done.10 = bf16[256,1024]{1,0:T(8,128)(2,1)S(1)} collective-permute-done((bf16[256,1024]{1,0:T(8,128)(2,1)S(1)}, bf16[256,1024]{1,0:T(8,128)(2,1)S(1)}, u32[]{:S(2)}, u32[]{:S(2)}) %collective-permute-start.10) | collective-permute-done | bytes 524320 | tf_op jit(solution)/shard_map/ppermute | solution.py:218
  80.1 1.3 convolution_convert_fusion.5.refs_22_
  81.4 1.3 convolution_convert_fusion.16.refs_10_
  82.7 6.8 %collective-permute-done.13 = bf16[256,1024]{1,0:T(8,128)(2,1)S(1)} collective-permute-done((bf16[256,1024]{1,0:T(8,128)(2,1)S(1)}, bf16[256,1024]{1,0:T(8,128)(2,1)S(1)}, u32[]{:S(2)}, u32[]{:S(2)}) %collective-permute-start.13) | collective-permute-done | bytes 524320 | tf_op jit(solution)/shard_map/ppermute | solution.py:218
  89.5 7.3 %collective-permute-start.11 = (bf16[512,1024]{1,0:T(8,128)(2,1)S(1)}, bf16[512,1024]{1,0:T(8,128)(2,1)S(1)}, u32[]{:S(2)}, u32[]{:S(2)}) collective-permute-start(bf16[512,1024]{1,0:T(8,128)(2,1)S(1)} %constant_dynamic-update-slice_fusion.4), channel_id=1, source_target_pairs={{0,1},{1,0},{2,3},{3,2},{4,5},{5,4},{6,7},{7,6},{8,9},{9,8},{10,11... | collective-permute-start | bytes 3145736 | tf_op jit(solution)/shard_map/ppermute | solution.py:219
  96.9 1.3 convolution_convert_fusion.3.refs_24_
  99.5 1.3 convolution_convert_fusion.12.refs_15_
  102.1 7.3 %collective-permute-start.3 = (bf16[512,1024]{1,0:T(8,128)(2,1)S(1)}, bf16[512,1024]{1,0:T(8,128)(2,1)S(1)}, u32[]{:S(2)}, u32[]{:S(2)}) collective-permute-start(bf16[512,1024]{1,0:T(8,128)(2,1)S(1)} %collective-permute-done.1), channel_id=1, source_target_pairs={{0,1},{9,8},{1,2},{10,9},{2,3},{11,10},{3,4},{12,11},{4,5},{13,12}... | collective-permute-start | bytes 3145736 | tf_op jit(solution)/shard_map/ppermute | solution.py:227
  109.4 1.3 convolution_convert_fusion.8.refs_19_
  111.9 1.3 convolution_convert_fusion.9.refs_18_
  114.5 1.3 convolution_convert_fusion.6.refs_21_
  117.1 1.3 convolution_convert_fusion.4.refs_23_
  119.6 1.3 convolution_convert_fusion.2.refs_25_
  122.2 1.3 convolution_convert_fusion.10.refs_17_
  123.5 1.5 convolution_convert_fusion.21.refs_5_
  125.0 58.0 %attend.1 = bf16[1024,1024]{1,0:T(8,128)(2,1)S(1)} custom-call(s32[8,16]{1,0:T(8,128)S(1)} %fusion.11.refs_0_, bf16[1024,1024]{1,0:T(8,128)(2,1)S(1)} %multiply_convert_fusion.refs_1_, bf16[1024,1024]{1,0:T(8,128)(2,1)S(1)} %convolution_convert_fusion.1.refs_2_, bf16[512,1024]{1,0:T(8,128)(2,1)S(1)} %convolution_convert_fusion.23.refs_3_, ...), custom_call_target="tpu_custom_call" | custom-call | flops 51539607552 | bytes 37748736 | tf_op jit(solution)/shard_map/attend/pallas_call | solution.py:188
  183.1 3.7 %convert_bitcast_fusion = bf16[1,1024,1024]{2,1,0:T(8,128)(2,1)} fusion(bf16[1024,1024]{1,0:T(8,128)(2,1)S(1)} %attend.1, bf16[1024,1024]{1,0:T(8,128)(2,1)S(1)} %copy-done), kind=kOutput, calls=%fused_computation.1 | convolution fusion | flops 2148532224 | bytes 6291456 | tf_op jit(solution)/shard_map/dot_general | solution.py:308
  (50 shorter events, 17.0 us)
Async XLA Ops:
  0.0 183.1 %copy-start = (bf16[1024,1024]{1,0:T(8,128)(2,1)S(1)}, bf16[1024,1024]{1,0:T(8,128)(2,1)}, u32[]{:S(2)}) copy-start(bf16[1024,1024]{1,0:T(8,128)(2,1)} %param.6) | copy-start | bytes 6291460
  1.2 12.9 %collective-permute-start = (bf16[256,1024]{1,0:T(8,128)(2,1)S(1)}, bf16[256,1024]{1,0:T(8,128)(2,1)S(1)}, u32[]{:S(2)}, u32[]{:S(2)}) collective-permute-start(bf16[256,1024]{1,0:T(8,128)(2,1)S(1)} %slice_bitcast_fusion), channel_id=1, source_target_pairs={{0,8},{8,0},{1,9},{9,1},{2,10},{10,2},{3,11},{11,3},{4,12},{12,4},... | collective-permute-start | bytes 1572872 | tf_op jit(solution)/shard_map/ppermute | solution.py:218
  2.5 8.6 %copy-start.2 = (s32[16,16]{1,0:T(8,128)S(1)}, s32[16,16]{1,0:T(8,128)}, u32[]{:S(2)}) copy-start(s32[16,16]{1,0:T(8,128)} %param.7) | copy-start | bytes 3076
  11.2 8.0 %copy-start.1 = (bf16[1,1024,1024]{2,1,0:T(8,128)(2,1)S(1)}, bf16[1,1024,1024]{2,1,0:T(8,128)(2,1)}, u32[]{:S(2)}) copy-start(bf16[1,1024,1024]{2,1,0:T(8,128)(2,1)} %param.4) | copy-start | bytes 6291460
  15.4 19.2 %collective-permute-start.6 = (bf16[256,1024]{1,0:T(8,128)(2,1)S(1)}, bf16[256,1024]{1,0:T(8,128)(2,1)S(1)}, u32[]{:S(2)}, u32[]{:S(2)}) collective-permute-start(bf16[256,1024]{1,0:T(8,128)(2,1)S(1)} %get-tuple-element.23), channel_id=1, source_target_pairs={{0,2},{1,3},{2,4},{3,5},{4,6},{5,7},{6,0},{7,1},{8,10},{9,11},{10,... | collective-permute-start | bytes 1572872 | tf_op jit(solution)/shard_map/ppermute | solution.py:222
  16.8 37.8 %collective-permute-start.9 = (bf16[256,1024]{1,0:T(8,128)(2,1)S(1)}, bf16[256,1024]{1,0:T(8,128)(2,1)S(1)}, u32[]{:S(2)}, u32[]{:S(2)}) collective-permute-start(bf16[256,1024]{1,0:T(8,128)(2,1)S(1)} %get-tuple-element.23), channel_id=1, source_target_pairs={{0,4},{1,5},{2,6},{3,7},{4,0},{5,1},{6,2},{7,3},{8,12},{9,13},{10,... | collective-permute-start | bytes 1572872 | tf_op jit(solution)/shard_map/ppermute | solution.py:222
  17.9 5.2 %copy-start.3 = (bf16[1024,1024]{1,0:T(8,128)(2,1)S(1)}, bf16[1024,1024]{1,0:T(8,128)(2,1)}, u32[]{:S(2)}) copy-start(bf16[1024,1024]{1,0:T(8,128)(2,1)} %get-tuple-element.20) | copy-start | bytes 6291460
  17.9 11.4 %collective-permute-start.2 = (bf16[256,1024]{1,0:T(8,128)(2,1)S(1)}, bf16[256,1024]{1,0:T(8,128)(2,1)S(1)}, u32[]{:S(2)}, u32[]{:S(2)}) collective-permute-start(bf16[256,1024]{1,0:T(8,128)(2,1)S(1)} %get-tuple-element.26), channel_id=1, source_target_pairs={{0,8},{8,0},{1,9},{9,1},{2,10},{10,2},{3,11},{11,3},{4,12},{12,4},... | collective-permute-start | bytes 1572872 | tf_op jit(solution)/shard_map/ppermute | solution.py:218
  23.1 2.4 %copy-start.5 = (bf16[1024,1024]{1,0:T(8,128)(2,1)S(1)}, bf16[1024,1024]{1,0:T(8,128)(2,1)}, u32[]{:S(2)}) copy-start(bf16[1024,1024]{1,0:T(8,128)(2,1)} %get-tuple-element.18) | copy-start | bytes 6291460
  29.4 6.5 %copy-start.4 = (bf16[1024,1024]{1,0:T(8,128)(2,1)S(1)}, bf16[1024,1024]{1,0:T(8,128)(2,1)}, u32[]{:S(2)}) copy-start(bf16[1024,1024]{1,0:T(8,128)(2,1)} %get-tuple-element.24) | copy-start | bytes 6291460
  29.6 82.4 %collective-permute-start.4 = (bf16[512,1024]{1,0:T(8,128)(2,1)S(1)}, bf16[512,1024]{1,0:T(8,128)(2,1)S(1)}, u32[]{:S(2)}, u32[]{:S(2)}) collective-permute-start(bf16[512,1024]{1,0:T(8,128)(2,1)S(1)} %constant_dynamic-update-slice_fusion), channel_id=1, source_target_pairs={{0,1},{9,8},{1,2},{10,9},{2,3},{11,10},{3,4},{12,11},{4,5},{13,12}... | collective-permute-start | bytes 3145736 | tf_op jit(solution)/shard_map/ppermute | solution.py:227
  34.7 31.4 %collective-permute-start.7 = (bf16[256,1024]{1,0:T(8,128)(2,1)S(1)}, bf16[256,1024]{1,0:T(8,128)(2,1)S(1)}, u32[]{:S(2)}, u32[]{:S(2)}) collective-permute-start(bf16[256,1024]{1,0:T(8,128)(2,1)S(1)} %collective-permute-done.6), channel_id=1, source_target_pairs={{0,8},{8,0},{1,9},{9,1},{2,10},{10,2},{3,11},{11,3},{4,12},{12,4},... | collective-permute-start | bytes 1572872 | tf_op jit(solution)/shard_map/ppermute | solution.py:218
  37.1 31.5 %collective-permute-start.12 = (bf16[256,1024]{1,0:T(8,128)(2,1)S(1)}, bf16[256,1024]{1,0:T(8,128)(2,1)S(1)}, u32[]{:S(2)}, u32[]{:S(2)}) collective-permute-start(bf16[256,1024]{1,0:T(8,128)(2,1)S(1)} %get-tuple-element.23), channel_id=1, source_target_pairs={{0,6},{1,7},{2,0},{3,1},{4,2},{5,3},{6,4},{7,5},{8,14},{9,15},{10,... | collective-permute-start | bytes 1572872 | tf_op jit(solution)/shard_map/ppermute | solution.py:222
  38.8 60.7 %collective-permute-start.1 = (bf16[512,1024]{1,0:T(8,128)(2,1)S(1)}, bf16[512,1024]{1,0:T(8,128)(2,1)S(1)}, u32[]{:S(2)}, u32[]{:S(2)}) collective-permute-start(bf16[512,1024]{1,0:T(8,128)(2,1)S(1)} %get-tuple-element.28), channel_id=1, source_target_pairs={{0,8},{8,0},{1,9},{9,1},{2,10},{10,2},{3,11},{11,3},{4,12},{12,4},... | collective-permute-start | bytes 3145736 | tf_op jit(solution)/shard_map/ppermute | solution.py:218
  54.5 47.6 %collective-permute-start.5 = (bf16[512,1024]{1,0:T(8,128)(2,1)S(1)}, bf16[512,1024]{1,0:T(8,128)(2,1)S(1)}, u32[]{:S(2)}, u32[]{:S(2)}) collective-permute-start(bf16[512,1024]{1,0:T(8,128)(2,1)S(1)} %get-tuple-element.27), channel_id=1, source_target_pairs={{0,1},{1,0},{2,3},{3,2},{4,5},{5,4},{6,7},{7,6},{8,9},{9,8},{10,11... | collective-permute-start | bytes 3145736 | tf_op jit(solution)/shard_map/ppermute | solution.py:219
  66.0 14.1 %collective-permute-start.10 = (bf16[256,1024]{1,0:T(8,128)(2,1)S(1)}, bf16[256,1024]{1,0:T(8,128)(2,1)S(1)}, u32[]{:S(2)}, u32[]{:S(2)}) collective-permute-start(bf16[256,1024]{1,0:T(8,128)(2,1)S(1)} %collective-permute-done.9), channel_id=1, source_target_pairs={{0,8},{8,0},{1,9},{9,1},{2,10},{10,2},{3,11},{11,3},{4,12},{12,4},... | collective-permute-start | bytes 1572872 | tf_op jit(solution)/shard_map/ppermute | solution.py:218
  68.7 45.8 %collective-permute-start.8 = (bf16[512,1024]{1,0:T(8,128)(2,1)S(1)}, bf16[512,1024]{1,0:T(8,128)(2,1)S(1)}, u32[]{:S(2)}, u32[]{:S(2)}) collective-permute-start(bf16[512,1024]{1,0:T(8,128)(2,1)S(1)} %constant_dynamic-update-slice_fusion.2), channel_id=1, source_target_pairs={{0,1},{1,0},{2,3},{3,2},{4,5},{5,4},{6,7},{7,6},{8,9},{9,8},{10,11... | collective-permute-start | bytes 3145736 | tf_op jit(solution)/shard_map/ppermute | solution.py:219
  80.1 9.4 %collective-permute-start.13 = (bf16[256,1024]{1,0:T(8,128)(2,1)S(1)}, bf16[256,1024]{1,0:T(8,128)(2,1)S(1)}, u32[]{:S(2)}, u32[]{:S(2)}) collective-permute-start(bf16[256,1024]{1,0:T(8,128)(2,1)S(1)} %collective-permute-done.12), channel_id=1, source_target_pairs={{0,8},{8,0},{1,9},{9,1},{2,10},{10,2},{3,11},{11,3},{4,12},{12,4},... | collective-permute-start | bytes 1572872 | tf_op jit(solution)/shard_map/ppermute | solution.py:218
  89.5 27.5 %collective-permute-start.11 = (bf16[512,1024]{1,0:T(8,128)(2,1)S(1)}, bf16[512,1024]{1,0:T(8,128)(2,1)S(1)}, u32[]{:S(2)}, u32[]{:S(2)}) collective-permute-start(bf16[512,1024]{1,0:T(8,128)(2,1)S(1)} %constant_dynamic-update-slice_fusion.4), channel_id=1, source_target_pairs={{0,1},{1,0},{2,3},{3,2},{4,5},{5,4},{6,7},{7,6},{8,9},{9,8},{10,11... | collective-permute-start | bytes 3145736 | tf_op jit(solution)/shard_map/ppermute | solution.py:219
  99.5 20.2 %collective-permute-start.14 = (bf16[512,1024]{1,0:T(8,128)(2,1)S(1)}, bf16[512,1024]{1,0:T(8,128)(2,1)S(1)}, u32[]{:S(2)}, u32[]{:S(2)}) collective-permute-start(bf16[512,1024]{1,0:T(8,128)(2,1)S(1)} %constant_dynamic-update-slice_fusion.6), channel_id=1, source_target_pairs={{0,1},{1,0},{2,3},{3,2},{4,5},{5,4},{6,7},{7,6},{8,9},{9,8},{10,11... | collective-permute-start | bytes 3145736 | tf_op jit(solution)/shard_map/ppermute | solution.py:219
  102.1 20.1 %collective-permute-start.3 = (bf16[512,1024]{1,0:T(8,128)(2,1)S(1)}, bf16[512,1024]{1,0:T(8,128)(2,1)S(1)}, u32[]{:S(2)}, u32[]{:S(2)}) collective-permute-start(bf16[512,1024]{1,0:T(8,128)(2,1)S(1)} %collective-permute-done.1), channel_id=1, source_target_pairs={{0,1},{9,8},{1,2},{10,9},{2,3},{11,10},{3,4},{12,11},{4,5},{13,12}... | collective-permute-start | bytes 3145736 | tf_op jit(solution)/shard_map/ppermute | solution.py:227
where the time goes:
time: 187 us
  Pallas kernels  66.6 us (36%)
  matrix products  40.6 us (22%)
  starting transfers between devices  38 us (20%)
  waiting for transfers between devices  38 us (20%)
    pallas_call x1, Pallas kernels, attend(): pl.pallas_call(functools.partial(attend_kernel, not state, last, blocks,...  58 us
    ppermute x6, waiting for transfers between devices, rows_by_axes(): swap = lambda rows: lax.ppermute(rows, 'head', [(0, 1), (1, 0)])  22.4 us
    dot_general x13, matrix products, project_columns(): lax.dot_general(weight, rows, (((1,), (1,)), ((), ())), preferred_element...  20.5 us
    ppermute x4, starting transfers between devices, rows_by_axes(): lax.ppermute(rows, 'blk', [(s, s ^ 1) for s in range(strides)])  17.6 us
    dot_general x12, matrix products, project_rows(): jnp.dot(rows, weight, preferred_element_type=jnp.float32)  16.5 us
    ppermute x3, waiting for transfers between devices, along(): lax.ppermute(rows, 'blk', [(s, (s + 2 * k) % strides) for s in range(stri...  15.6 us
    ppermute x2, starting transfers between devices, rows_by_axes(): to_next = lambda rows: lax.ppermute(rows, ('head', 'blk'), steps)  12.3 us
    pallas_call x1, Pallas kernels, split_weights(): pl.pallas_call(split_kernel, grid=(PAIRS,), in_specs=[pl.BlockSpec((D, 3...  8.61 us
  transfers between devices with their start and end apart: 15, of which 5 were waited for; matrix products, arithmetic and copies ran while one was open for 19% of the time, Pallas kernels for 5%

commit v1 on v0

--- a/solution.py
+++ b/solution.py
@@ -226,21 +226,19 @@
         steps += [(s, s + 1), (strides + s + 1, strides + s)]
     to_next = lambda rows: lax.ppermute(rows, ("head", "blk"), steps)
 
-    other_mid = swap(own[cut : cut + half])
-    other_mid, own, weights = lax.optimization_barrier((other_mid, own, weights))
-    carried = jnp.where(low, other_mid, own[cut + half :])
-    other_low, other_top = swap(own[:cut]), swap(own[cut + half :])
+    other_end = swap(own[-half:])
+    other_end, own, weights = lax.optimization_barrier((other_end, own, weights))
+    carried = jnp.where(low, other_end, own[cut : cut + half])
+    other = swap(own[:-half])
     slots = [None] * chips
     slots[2:-1] = [along(carried, k) for k in range(2, chips - 1)]
     slots[1] = along(carried, 1)
-    slots[1], carried = lax.optimization_barrier((slots[1], carried))
-    slots[-1] = along(carried, chips - 1)
-    slots = [jnp.concatenate([rows, swap(rows)], axis=0) for rows in slots[1:]]
-    other_high = jnp.concatenate([other_mid, other_top], axis=0)
-    edge_low = to_next(other_low)
-    edge_high = to_next(other_high)
-    pieces = [own, other_low, other_high, edge_low, edge_high, beside(jnp.where(low, other_high, own[cut:]))]
-    for rows in slots:
+    slots[1], after = lax.optimization_barrier((slots[1], carried))
+    slots[-1] = along(after, chips - 1)
+    slots[0] = jnp.concatenate([carried, jnp.where(low, other[-half:], own[-half:])], axis=0)
+    slots[1:] = [jnp.concatenate([rows, swap(rows)], axis=0) for rows in slots[1:]]
+    pieces = [own, other, other_end, to_next(other), to_next(other_end), beside(slots[0])]
+    for rows in slots[1:]:
         pieces += [rows, beside(rows)]
 
     def position(block):
@@ -250,9 +248,8 @@
         edge = jnp.where(rel < 0, rel + SB + 8, rel)
         order = inside - (SB - SUMB)
         k = (stride // 2 - of // 2) % chips
-        turned = (order // 2 ^ place) * 2 + order % 2
-        far = 28 + (k - 1) * 8 + jnp.where(of % 2 == stride % 2, 0, 4) + turned
-        far = jnp.where(k == 0, 24 + order, far)
+        turned = (order // 2 ^ (1 - place)) * 2 + order % 2
+        far = jnp.where(k == 0, 24, 28 + (k - 1) * 8 + jnp.where(of % 2 == stride % 2, 0, 4)) + turned
         return jnp.where(of == stride, mine, edge), jnp.where(of == stride, mine, far)
 
     return pieces, weights, position
@@ -304,7 +301,7 @@
     query = project_columns(query_weight, own, HD**-0.5)
     keys = [project_rows(rows, key_weight) for rows in pieces]
     values = [project_columns(value_weight, rows) for rows in pieces]
-    mixed = attend("attend", table, query, keys, values, [], True, 2, 4)
+    mixed = attend("attend", table, query, keys, values, [], True, 2, 8)
     out = jnp.dot(mixed, out_weight, preferred_element_type=jnp.float32).astype(jnp.bfloat16)
     return out.reshape(tokens.shape)
 

time: 187 us -> 227 us (1.21)
  waiting for transfers between devices: 38 us -> 84.7 us
  starting transfers between devices: 38 us -> 24 us
  Pallas kernels: 66.6 us -> 72 us
  local copies, waits for them, and re-layouts: 1.5 us -> 3.88 us
    ppermute x6 -> x5, waiting for transfers between devices: 22.4 us -> 53.5 us  [rows_by_axes(): swap = lambda rows: lax.ppermute(rows, 'head', [(0, 1), (1, 0)])]
    ppermute x3, waiting for transfers between devices: 15.6 us -> 31.2 us  [along(): lax.ppermute(rows, 'blk', [(s, (s + 2 * k) % strides) for s in range(stri...]
    ppermute x4, starting transfers between devices: 17.6 us -> 4.18 us  [rows_by_axes(): lax.ppermute(rows, 'blk', [(s, s ^ 1) for s in range(strides)])]
    ppermute x6 -> x5, starting transfers between devices: 3.98 us -> 11.2 us  [rows_by_axes(): swap = lambda rows: lax.ppermute(rows, 'head', [(0, 1), (1, 0)])]
    pallas_call x1, Pallas kernels: 58 us -> 63.4 us  [attend(): pl.pallas_call(functools.partial(attend_kernel, not state, last, blocks,...]
    ppermute x2, starting transfers between devices: 12.3 us -> 7.18 us  [rows_by_axes(): to_next = lambda rows: lax.ppermute(rows, ('head', 'blk'), steps)]
    ppermute x3, starting transfers between devices: 4.06 us -> 1.43 us  [along(): lax.ppermute(rows, 'blk', [(s, (s + 2 * k) % strides) for s in range(stri...]
    unnamed x15, local copies, waits for them, and re-layouts: 0.13 us -> 2.43 us
  transfers between devices with their start and end apart: 15 -> 14, of which waited for: 5 -> 6; matrix products, arithmetic and copies ran while one was open for 19% -> 15% of each run, Pallas kernels for 5% -> 4%
where the time goes in v1:
time: 227 us; the launch traced here: 226 us
  waiting for transfers between devices  84.7 us (37%)
  Pallas kernels  72 us (32%)
  matrix products  40.6 us (18%)
  starting transfers between devices  24 us (11%)
  local copies, waits for them, and re-layouts  3.88 us (2%)
    pallas_call x1, Pallas kernels, attend(): pl.pallas_call(functools.partial(attend_kernel, not state, last, blocks,...  63.4 us
    ppermute x5, waiting for transfers between devices, rows_by_axes(): swap = lambda rows: lax.ppermute(rows, 'head', [(0, 1), (1, 0)])  53.5 us
    ppermute x3, waiting for transfers between devices, along(): lax.ppermute(rows, 'blk', [(s, (s + 2 * k) % strides) for s in range(stri...  31.2 us
    dot_general x13, matrix products, project_columns(): lax.dot_general(weight, rows, (((1,), (1,)), ((), ())), preferred_element...  20.7 us
    dot_general x12, matrix products, project_rows(): jnp.dot(rows, weight, preferred_element_type=jnp.float32)  16.2 us
    ppermute x5, starting transfers between devices, rows_by_axes(): swap = lambda rows: lax.ppermute(rows, 'head', [(0, 1), (1, 0)])  11.2 us
    pallas_call x1, Pallas kernels, split_weights(): pl.pallas_call(split_kernel, grid=(PAIRS,), in_specs=[pl.BlockSpec((D, 3...  8.6 us
    ppermute x2, starting transfers between devices, rows_by_axes(): to_next = lambda rows: lax.ppermute(rows, ('head', 'blk'), steps)  7.18 us
  transfers between devices with their start and end apart: 14, of which 6 were waited for; matrix products, arithmetic and copies ran while one was open for 15% of the time, Pallas kernels for 4%

profile of v1, /device:TPU:11, one launch (start us, length us, event | category | flops | bytes accessed | tf_op | source)
XLA Modules:
  0.0 225.8 jit_solution(14898006828373181104)
XLA Ops:
  1.2 1.3 collective-permute-start
  2.5 8.6 %split_weights.1 = (bf16[1024,1024]{1,0:T(8,128)(2,1)}, bf16[1024,1024]{1,0:T(8,128)(2,1)}, bf16[1024,1024]{1,0:T(8,128)(2,1)}) custom-call(bf16[1024,3072]{1,0:T(8,128)(2,1)} %weight_ref.1), custom_call_target="tpu_custom_call" | custom-call | bytes 12582912 | tf_op jit(solution)/shard_map/split_weights/pallas_call | solution.py:41
  11.2 2.9 %collective-permute-done = bf16[256,1024]{1,0:T(8,128)(2,1)S(1)} collective-permute-done((bf16[256,1024]{1,0:T(8,128)(2,1)S(1)}, bf16[256,1024]{1,0:T(8,128)(2,1)S(1)}, u32[]{:S(2)}, u32[]{:S(2)}) %collective-permute-start) | collective-permute-done | bytes 524320 | tf_op jit(solution)/shard_map/ppermute | solution.py:218
  14.1 4.8 %collective-permute-start.3 = (bf16[256,1024]{1,0:T(8,128)(2,1)S(1)}, bf16[256,1024]{1,0:T(8,128)(2,1)S(1)}, u32[]{:S(2)}, u32[]{:S(2)}) collective-permute-start(bf16[256,1024]{1,0:T(8,128)(2,1)S(1)} %collective-permute-done), channel_id=1, source_target_pairs={{0,1},{9,8},{1,2},{10,9},{2,3},{11,10},{3,4},{12,11},{4,5},{13,12}... | collective-permute-start | bytes 1572872 | tf_op jit(solution)/shard_map/ppermute | solution.py:227
  18.9 2.3 %convolution_convert_fusion.21.refs_16_ = bf16[1024,256]{1,0:T(8,128)(2,1)S(1)} fusion(bf16[1024,1024]{1,0:T(8,128)(2,1)} %get-tuple-element.24, bf16[256,1024]{1,0:T(8,128)(2,1)S(1)} %collective-permute-done), kind=kOutput, calls=%fused_computation.23 | convolution fusion | flops 537133056 | bytes 3145728 | tf_op jit(solution)/shard_map/dot_general | solution.py:208
  21.4 1.5 copy-done.4
  22.8 2.4 %convolution_convert_fusion.refs_14_ = bf16[1024,1024]{1,0:T(8,128)(2,1)S(1)} fusion(bf16[1024,1024]{1,0:T(8,128)(2,1)S(1)} %copy-done.4, bf16[1024,1024]{1,0:T(8,128)(2,1)S(1)} %bitcast.58), kind=kOutput, calls=%fused_computation.2 | convolution fusion | flops 2148532224 | bytes 6291456 | tf_op jit(solution)/shard_map/dot_general | solution.py:208
  25.3 2.3 %convolution_convert_fusion.1.refs_2_ = bf16[1024,1024]{1,0:T(8,128)(2,1)S(1)} fusion(bf16[1024,1024]{1,0:T(8,128)(2,1)S(1)} %bitcast.59, bf16[1024,1024]{1,0:T(8,128)(2,1)S(1)} %copy-done.3), kind=kOutput, calls=%fused_computation.3 | convolution fusion | flops 2148532224 | bytes 6291456 | tf_op jit(solution)/shard_map/dot_general | solution.py:204
  29.3 2.4 %multiply_convert_fusion.refs_1_ = bf16[1024,1024]{1,0:T(8,128)(2,1)S(1)} fusion(bf16[1024,1024]{1,0:T(8,128)(2,1)S(1)} %copy-done.5, bf16[1024,1024]{1,0:T(8,128)(2,1)S(1)} %bitcast.60), kind=kOutput, calls=%fused_computation | convolution fusion | flops 2149580800 | bytes 6291456 | tf_op jit(solution)/shard_map/dot_general | solution.py:208
  33.1 27.6 %collective-permute-done.1 = bf16[768,1024]{1,0:T(8,128)(2,1)S(1)} collective-permute-done((bf16[768,1024]{1,0:T(8,128)(2,1)S(1)}, bf16[768,1024]{1,0:T(8,128)(2,1)S(1)}, u32[]{:S(2)}, u32[]{:S(2)}) %collective-permute-start.1) | collective-permute-done | bytes 1572896 | tf_op jit(solution)/shard_map/ppermute | solution.py:218
  60.8 1.4 collective-permute-start.8
  62.3 1.3 collective-permute-start.4
  63.7 1.8 convolution_convert_fusion.3.refs_15_
  65.5 2.4 %collective-permute-start.2 = (bf16[768,1024]{1,0:T(8,128)(2,1)S(1)}, bf16[768,1024]{1,0:T(8,128)(2,1)S(1)}, u32[]{:S(2)}, u32[]{:S(2)}) collective-permute-start(bf16[768,1024]{1,0:T(8,128)(2,1)S(1)} %collective-permute-done.1), channel_id=1, source_target_pairs={{0,1},{9,8},{1,2},{10,9},{2,3},{11,10},{3,4},{12,11},{4,5},{13,12}... | collective-permute-start | bytes 4718600 | tf_op jit(solution)/shard_map/ppermute | solution.py:227
  67.9 1.8 convolution_convert_fusion.5.refs_3_
  69.7 31.2 %collective-permute-done.5 = bf16[256,1024]{1,0:T(8,128)(2,1)S(1)} collective-permute-done((bf16[256,1024]{1,0:T(8,128)(2,1)S(1)}, bf16[256,1024]{1,0:T(8,128)(2,1)S(1)}, u32[]{:S(2)}, u32[]{:S(2)}) %collective-permute-start.5) | collective-permute-done | bytes 524320 | tf_op jit(solution)/shard_map/ppermute | solution.py:222
  100.9 8.2 %collective-permute-start.6 = (bf16[256,1024]{1,0:T(8,128)(2,1)S(1)}, bf16[256,1024]{1,0:T(8,128)(2,1)S(1)}, u32[]{:S(2)}, u32[]{:S(2)}) collective-permute-start(bf16[256,1024]{1,0:T(8,128)(2,1)S(1)} %collective-permute-done.5), channel_id=1, source_target_pairs={{0,8},{8,0},{1,9},{9,1},{2,10},{10,2},{3,11},{11,3},{4,12},{12,4},... | collective-permute-start | bytes 1572872 | tf_op jit(solution)/shard_map/ppermute | solution.py:218
  109.3 1.3 convolution_convert_fusion.12.refs_19_
  111.8 9.1 %collective-permute-done.6 = bf16[256,1024]{1,0:T(8,128)(2,1)S(1)} collective-permute-done((bf16[256,1024]{1,0:T(8,128)(2,1)S(1)}, bf16[256,1024]{1,0:T(8,128)(2,1)S(1)}, u32[]{:S(2)}, u32[]{:S(2)}) %collective-permute-start.6) | collective-permute-done | bytes 524320 | tf_op jit(solution)/shard_map/ppermute | solution.py:218
  121.0 1.3 convolution_convert_fusion.11.refs_20_
  122.3 1.6 collective-permute-start.12
  123.8 8.3 %collective-permute-done.9 = bf16[256,1024]{1,0:T(8,128)(2,1)S(1)} collective-permute-done((bf16[256,1024]{1,0:T(8,128)(2,1)S(1)}, bf16[256,1024]{1,0:T(8,128)(2,1)S(1)}, u32[]{:S(2)}, u32[]{:S(2)}) %collective-permute-start.9) | collective-permute-done | bytes 524320 | tf_op jit(solution)/shard_map/ppermute | solution.py:218
  133.5 1.3 convolution_convert_fusion.9.refs_22_
  134.8 1.7 collective-permute-start.10
  137.9 5.6 %collective-permute-done.12 = bf16[256,1024]{1,0:T(8,128)(2,1)S(1)} collective-permute-done((bf16[256,1024]{1,0:T(8,128)(2,1)S(1)}, bf16[256,1024]{1,0:T(8,128)(2,1)S(1)}, u32[]{:S(2)}, u32[]{:S(2)}) %collective-permute-start.12) | collective-permute-done | bytes 524320 | tf_op jit(solution)/shard_map/ppermute | solution.py:218
  144.5 1.8 convolution_convert_fusion.2.refs_17_
  147.7 1.8 convolution_convert_fusion.4.refs_5_
  150.8 1.5 convolution_convert_fusion.8.refs_23_
  153.5 1.3 convolution_convert_fusion.10.refs_21_
  156.1 1.3 convolution_convert_fusion.6.refs_25_
  158.7 63.4 %attend.1 = bf16[1024,1024]{1,0:T(8,128)(2,1)S(1)} custom-call(s32[8,16]{1,0:T(8,128)S(1)} %fusion.10.refs_0_, bf16[1024,1024]{1,0:T(8,128)(2,1)S(1)} %multiply_convert_fusion.refs_1_, bf16[1024,1024]{1,0:T(8,128)(2,1)S(1)} %convolution_convert_fusion.1.refs_2_, bf16[768,1024]{1,0:T(8,128)(2,1)S(1)} %convolution_convert_fusion.5.refs_3_, ...), custom_call_target="tpu_custom_call" | custom-call | flops 51539607552 | bytes 37748736 | tf_op jit(solution)/shard_map/attend/pallas_call | solution.py:188
  222.1 3.7 %convert_bitcast_fusion = bf16[1,1024,1024]{2,1,0:T(8,128)(2,1)} fusion(bf16[1024,1024]{1,0:T(8,128)(2,1)S(1)} %attend.1, bf16[1024,1024]{1,0:T(8,128)(2,1)S(1)} %copy-done), kind=kOutput, calls=%fused_computation.1 | convolution fusion | flops 2148532224 | bytes 6291456 | tf_op jit(solution)/shard_map/dot_general | solution.py:305
  (48 shorter events, 16.4 us)
Async XLA Ops:
  0.0 222.1 %copy-start = (bf16[1024,1024]{1,0:T(8,128)(2,1)S(1)}, bf16[1024,1024]{1,0:T(8,128)(2,1)}, u32[]{:S(2)}) copy-start(bf16[1024,1024]{1,0:T(8,128)(2,1)} %param.6) | copy-start | bytes 6291460
  1.2 12.9 %collective-permute-start = (bf16[256,1024]{1,0:T(8,128)(2,1)S(1)}, bf16[256,1024]{1,0:T(8,128)(2,1)S(1)}, u32[]{:S(2)}, u32[]{:S(2)}) collective-permute-start(bf16[256,1024]{1,0:T(8,128)(2,1)S(1)} %slice_bitcast_fusion), channel_id=1, source_target_pairs={{0,8},{8,0},{1,9},{9,1},{2,10},{10,2},{3,11},{11,3},{4,12},{12,4},... | collective-permute-start | bytes 1572872 | tf_op jit(solution)/shard_map/ppermute | solution.py:218
  2.5 8.6 %copy-start.2 = (s32[16,16]{1,0:T(8,128)S(1)}, s32[16,16]{1,0:T(8,128)}, u32[]{:S(2)}) copy-start(s32[16,16]{1,0:T(8,128)} %param.7) | copy-start | bytes 3076
  14.1 7.1 %copy-start.1 = (bf16[1,1024,1024]{2,1,0:T(8,128)(2,1)S(1)}, bf16[1,1024,1024]{2,1,0:T(8,128)(2,1)}, u32[]{:S(2)}) copy-start(bf16[1,1024,1024]{2,1,0:T(8,128)(2,1)} %param.4) | copy-start | bytes 6291460
  14.1 17.5 %collective-permute-start.3 = (bf16[256,1024]{1,0:T(8,128)(2,1)S(1)}, bf16[256,1024]{1,0:T(8,128)(2,1)S(1)}, u32[]{:S(2)}, u32[]{:S(2)}) collective-permute-start(bf16[256,1024]{1,0:T(8,128)(2,1)S(1)} %collective-permute-done), channel_id=1, source_target_pairs={{0,1},{9,8},{1,2},{10,9},{2,3},{11,10},{3,4},{12,11},{4,5},{13,12}... | collective-permute-start | bytes 1572872 | tf_op jit(solution)/shard_map/ppermute | solution.py:227
  21.2 1.6 copy-start.4
  22.8 2.5 %copy-start.3 = (bf16[1024,1024]{1,0:T(8,128)(2,1)S(1)}, bf16[1024,1024]{1,0:T(8,128)(2,1)}, u32[]{:S(2)}) copy-start(bf16[1024,1024]{1,0:T(8,128)(2,1)} %get-tuple-element.20) | copy-start | bytes 6291460
  25.2 35.5 %collective-permute-start.1 = (bf16[768,1024]{1,0:T(8,128)(2,1)S(1)}, bf16[768,1024]{1,0:T(8,128)(2,1)S(1)}, u32[]{:S(2)}, u32[]{:S(2)}) collective-permute-start(bf16[768,1024]{1,0:T(8,128)(2,1)S(1)} %slice.20), channel_id=1, source_target_pairs={{0,8},{8,0},{1,9},{9,1},{2,10},{10,2},{3,11},{11,3},{4,12},{12,4},... | collective-permute-start | bytes 4718600 | tf_op jit(solution)/shard_map/ppermute | solution.py:218
  27.7 1.6 copy-start.5
  60.8 48.3 %collective-permute-start.8 = (bf16[256,1024]{1,0:T(8,128)(2,1)S(1)}, bf16[256,1024]{1,0:T(8,128)(2,1)S(1)}, u32[]{:S(2)}, u32[]{:S(2)}) collective-permute-start(bf16[256,1024]{1,0:T(8,128)(2,1)S(1)} %get-tuple-element.23), channel_id=1, source_target_pairs={{0,4},{1,5},{2,6},{3,7},{4,0},{5,1},{6,2},{7,3},{8,12},{9,13},{10,... | collective-permute-start | bytes 1572872 | tf_op jit(solution)/shard_map/ppermute | solution.py:222
  62.2 38.7 %collective-permute-start.5 = (bf16[256,1024]{1,0:T(8,128)(2,1)S(1)}, bf16[256,1024]{1,0:T(8,128)(2,1)S(1)}, u32[]{:S(2)}, u32[]{:S(2)}) collective-permute-start(bf16[256,1024]{1,0:T(8,128)(2,1)S(1)} %get-tuple-element.23), channel_id=1, source_target_pairs={{0,2},{1,3},{2,4},{3,5},{4,6},{5,7},{6,0},{7,1},{8,10},{9,11},{10,... | collective-permute-start | bytes 1572872 | tf_op jit(solution)/shard_map/ppermute | solution.py:222
  62.3 46.9 %collective-permute-start.4 = (bf16[512,1024]{1,0:T(8,128)(2,1)S(1)}, bf16[512,1024]{1,0:T(8,128)(2,1)S(1)}, u32[]{:S(2)}, u32[]{:S(2)}) collective-permute-start(bf16[512,1024]{1,0:T(8,128)(2,1)S(1)} %pad_maximum_fusion), channel_id=1, source_target_pairs={{0,1},{1,0},{2,3},{3,2},{4,5},{5,4},{6,7},{7,6},{8,9},{9,8},{10,11... | collective-permute-start | bytes 3145736 | tf_op jit(solution)/shard_map/ppermute | solution.py:219
  65.5 79.1 %collective-permute-start.2 = (bf16[768,1024]{1,0:T(8,128)(2,1)S(1)}, bf16[768,1024]{1,0:T(8,128)(2,1)S(1)}, u32[]{:S(2)}, u32[]{:S(2)}) collective-permute-start(bf16[768,1024]{1,0:T(8,128)(2,1)S(1)} %collective-permute-done.1), channel_id=1, source_target_pairs={{0,1},{9,8},{1,2},{10,9},{2,3},{11,10},{3,4},{12,11},{4,5},{13,12}... | collective-permute-start | bytes 4718600 | tf_op jit(solution)/shard_map/ppermute | solution.py:227
  100.9 21.4 %collective-permute-start.11 = (bf16[256,1024]{1,0:T(8,128)(2,1)S(1)}, bf16[256,1024]{1,0:T(8,128)(2,1)S(1)}, u32[]{:S(2)}, u32[]{:S(2)}) collective-permute-start(bf16[256,1024]{1,0:T(8,128)(2,1)S(1)} %get-tuple-element.23), channel_id=1, source_target_pairs={{0,6},{1,7},{2,0},{3,1},{4,2},{5,3},{6,4},{7,5},{8,14},{9,15},{10,... | collective-permute-start | bytes 1572872 | tf_op jit(solution)/shard_map/ppermute | solution.py:222
  100.9 20.0 %collective-permute-start.6 = (bf16[256,1024]{1,0:T(8,128)(2,1)S(1)}, bf16[256,1024]{1,0:T(8,128)(2,1)S(1)}, u32[]{:S(2)}, u32[]{:S(2)}) collective-permute-start(bf16[256,1024]{1,0:T(8,128)(2,1)S(1)} %collective-permute-done.5), channel_id=1, source_target_pairs={{0,8},{8,0},{1,9},{9,1},{2,10},{10,2},{3,11},{11,3},{4,12},{12,4},... | collective-permute-start | bytes 1572872 | tf_op jit(solution)/shard_map/ppermute | solution.py:218
  109.1 23.1 %collective-permute-start.9 = (bf16[256,1024]{1,0:T(8,128)(2,1)S(1)}, bf16[256,1024]{1,0:T(8,128)(2,1)S(1)}, u32[]{:S(2)}, u32[]{:S(2)}) collective-permute-start(bf16[256,1024]{1,0:T(8,128)(2,1)S(1)} %collective-permute-done.8), channel_id=1, source_target_pairs={{0,8},{8,0},{1,9},{9,1},{2,10},{10,2},{3,11},{11,3},{4,12},{12,4},... | collective-permute-start | bytes 1572872 | tf_op jit(solution)/shard_map/ppermute | solution.py:218
  122.3 21.1 %collective-permute-start.12 = (bf16[256,1024]{1,0:T(8,128)(2,1)S(1)}, bf16[256,1024]{1,0:T(8,128)(2,1)S(1)}, u32[]{:S(2)}, u32[]{:S(2)}) collective-permute-start(bf16[256,1024]{1,0:T(8,128)(2,1)S(1)} %collective-permute-done.11), channel_id=1, source_target_pairs={{0,8},{8,0},{1,9},{9,1},{2,10},{10,2},{3,11},{11,3},{4,12},{12,4},... | collective-permute-start | bytes 1572872 | tf_op jit(solution)/shard_map/ppermute | solution.py:218
  134.8 16.0 %collective-permute-start.10 = (bf16[512,1024]{1,0:T(8,128)(2,1)S(1)}, bf16[512,1024]{1,0:T(8,128)(2,1)S(1)}, u32[]{:S(2)}, u32[]{:S(2)}) collective-permute-start(bf16[512,1024]{1,0:T(8,128)(2,1)S(1)} %constant_dynamic-update-slice_fusion.2), channel_id=1, source_target_pairs={{0,1},{1,0},{2,3},{3,2},{4,5},{5,4},{6,7},{7,6},{8,9},{9,8},{10,11... | collective-permute-start | bytes 3145736 | tf_op jit(solution)/shard_map/ppermute | solution.py:219
  136.5 17.1 %collective-permute-start.7 = (bf16[512,1024]{1,0:T(8,128)(2,1)S(1)}, bf16[512,1024]{1,0:T(8,128)(2,1)S(1)}, u32[]{:S(2)}, u32[]{:S(2)}) collective-permute-start(bf16[512,1024]{1,0:T(8,128)(2,1)S(1)} %constant_dynamic-update-slice_fusion), channel_id=1, source_target_pairs={{0,1},{1,0},{2,3},{3,2},{4,5},{5,4},{6,7},{7,6},{8,9},{9,8},{10,11... | collective-permute-start | bytes 3145736 | tf_op jit(solution)/shard_map/ppermute | solution.py:219
  143.5 12.6 %collective-permute-start.13 = (bf16[512,1024]{1,0:T(8,128)(2,1)S(1)}, bf16[512,1024]{1,0:T(8,128)(2,1)S(1)}, u32[]{:S(2)}, u32[]{:S(2)}) collective-permute-start(bf16[512,1024]{1,0:T(8,128)(2,1)S(1)} %constant_dynamic-update-slice_fusion.4), channel_id=1, source_target_pairs={{0,1},{1,0},{2,3},{3,2},{4,5},{5,4},{6,7},{7,6},{8,9},{9,8},{10,11... | collective-permute-start | bytes 3145736 | tf_op jit(solution)/shard_map/ppermute | solution.py:219

commit v2 on v1

--- a/solution.py
+++ b/solution.py
@@ -121,18 +121,6 @@
             row_out_ref[0, 1:2, at(index, 2 * BLK)] = count_all
         return count_all
 
-    def one(index):
-        query = queries(index)
-        total = None
-        shift = None if first else row_in_ref[0, 0:1, at(index, 2 * BLK)]
-        for which in range(0, count, chunk):
-            scores = score(index, which, query)
-            if shift is None:
-                shift = jnp.max(scores, axis=0, keepdims=True)
-            part = gather(values(index, which), jnp.exp(scores - shift).astype(bf16))
-            total = part if total is None else total + part
-        return finish(index, shift, total)
-
     def whole_row(index):
         query = queries(index)
         shift = jnp.full((1, 2 * BLK), -jnp.inf, f32) if first else row_in_ref[0, 0:1, at(index, 2 * BLK)]
@@ -151,8 +139,26 @@
         finish(index, shift, total, None if first else jnp.exp(old - shift))
 
     def body(number, peak):
-        for n in range(together):
-            peak = jnp.maximum(peak, one(number * together + n))
+        steps = [(number * together + n, which) for n in range(together) for which in range(0, count, chunk)]
+        asked = {}
+
+        def ask(index, which):
+            if which == 0:
+                asked["query"] = queries(index)
+            return score(index, which, asked["query"])
+
+        following = ask(*steps[0])
+        for number, (index, which) in enumerate(steps):
+            scores = following
+            if number + 1 < len(steps):
+                following = ask(*steps[number + 1])
+            if which == 0:
+                total = None
+                shift = jnp.max(scores, axis=0, keepdims=True) if first else row_in_ref[0, 0:1, at(index, 2 * BLK)]
+            part = gather(values(index, which), jnp.exp(scores - shift).astype(bf16))
+            total = part if total is None else total + part
+            if which + chunk == count:
+                peak = jnp.maximum(peak, finish(index, shift, total))
         return peak
 
     peak = lax.fori_loop(0, blocks // together, body, jnp.zeros((1, 2 * BLK), f32))
@@ -228,14 +234,14 @@
 
     other_end = swap(own[-half:])
     other_end, own, weights = lax.optimization_barrier((other_end, own, weights))
-    carried = jnp.where(low, other_end, own[cut : cut + half])
+    carried = lax.optimization_barrier(jnp.where(low, other_end, own[cut : cut + half]))
     other = swap(own[:-half])
     slots = [None] * chips
     slots[2:-1] = [along(carried, k) for k in range(2, chips - 1)]
     slots[1] = along(carried, 1)
-    slots[1], after = lax.optimization_barrier((slots[1], carried))
+    slots[1], other, after = lax.optimization_barrier((slots[1], other, carried))
     slots[-1] = along(after, chips - 1)
-    slots[0] = jnp.concatenate([carried, jnp.where(low, other[-half:], own[-half:])], axis=0)
+    slots[0] = jnp.where(low, jnp.concatenate([other_end, other[-half:]], axis=0), own[cut:])
     slots[1:] = [jnp.concatenate([rows, swap(rows)], axis=0) for rows in slots[1:]]
     pieces = [own, other, other_end, to_next(other), to_next(other_end), beside(slots[0])]
     for rows in slots[1:]:
@@ -301,7 +307,7 @@
     query = project_columns(query_weight, own, HD**-0.5)
     keys = [project_rows(rows, key_weight) for rows in pieces]
     values = [project_columns(value_weight, rows) for rows in pieces]
-    mixed = attend("attend", table, query, keys, values, [], True, 2, 8)
+    mixed = attend("attend", table, query, keys, values, [], True, 2, 4)
     out = jnp.dot(mixed, out_weight, preferred_element_type=jnp.float32).astype(jnp.bfloat16)
     return out.reshape(tokens.shape)
 

time: 227 us -> 210 us (0.925)
  the two profiles are of different devices: /device:TPU:11 before, /device:TPU:1 now
where the time goes in v2:
time: 210 us; the launch traced here: 209 us
  waiting for transfers between devices  72 us (34%)
  Pallas kernels  70.1 us (33%)
  matrix products  39.1 us (19%)
  starting transfers between devices  22.1 us (11%)
  local copies, waits for them, and re-layouts  3.85 us (2%)
    pallas_call x1, Pallas kernels, attend(): pl.pallas_call(functools.partial(attend_kernel, not state, last, blocks,...  61.5 us
    ppermute x3, waiting for transfers between devices, along(): lax.ppermute(rows, 'blk', [(s, (s + 2 * k) % strides) for s in range(stri...  37.7 us
    ppermute x5, waiting for transfers between devices, rows_by_axes(): swap = lambda rows: lax.ppermute(rows, 'head', [(0, 1), (1, 0)])  34.3 us
    dot_general x13, matrix products, project_columns(): lax.dot_general(weight, rows, (((1,), (1,)), ((), ())), preferred_element...  19.1 us
    dot_general x12, matrix products, project_rows(): jnp.dot(rows, weight, preferred_element_type=jnp.float32)  16.4 us
    pallas_call x1, Pallas kernels, split_weights(): pl.pallas_call(split_kernel, grid=(PAIRS,), in_specs=[pl.BlockSpec((D, 3...  8.61 us
    ppermute x5, starting transfers between devices, rows_by_axes(): swap = lambda rows: lax.ppermute(rows, 'head', [(0, 1), (1, 0)])  6.08 us
    ppermute x2, starting transfers between devices, rows_by_axes(): to_next = lambda rows: lax.ppermute(rows, ('head', 'blk'), steps)  5.74 us
  transfers between devices with their start and end apart: 14, of which 6 were waited for; matrix products, arithmetic and copies ran while one was open for 17% of the time, Pallas kernels for 4%

profile of v2, /device:TPU:1, one launch (start us, length us, event | category | flops | bytes accessed | tf_op | source)
XLA Modules:
  0.0 209.4 jit_solution(8824964725486101369)
XLA Ops:
  1.2 2.1 %collective-permute-start = (bf16[256,1024]{1,0:T(8,128)(2,1)S(1)}, bf16[256,1024]{1,0:T(8,128)(2,1)S(1)}, u32[]{:S(2)}, u32[]{:S(2)}) collective-permute-start(bf16[256,1024]{1,0:T(8,128)(2,1)S(1)} %slice_bitcast_fusion), channel_id=1, source_target_pairs={{0,8},{8,0},{1,9},{9,1},{2,10},{10,2},{3,11},{11,3},{4,12},{12,4},... | collective-permute-start | bytes 1572872 | tf_op jit(solution)/shard_map/ppermute | solution.py:224
  3.4 8.6 %split_weights.1 = (bf16[1024,1024]{1,0:T(8,128)(2,1)}, bf16[1024,1024]{1,0:T(8,128)(2,1)}, bf16[1024,1024]{1,0:T(8,128)(2,1)}) custom-call(bf16[1024,3072]{1,0:T(8,128)(2,1)} %weight_ref.1), custom_call_target="tpu_custom_call" | custom-call | bytes 12582912 | tf_op jit(solution)/shard_map/split_weights/pallas_call | solution.py:41
  12.0 3.0 %collective-permute-done = bf16[256,1024]{1,0:T(8,128)(2,1)S(1)} collective-permute-done((bf16[256,1024]{1,0:T(8,128)(2,1)S(1)}, bf16[256,1024]{1,0:T(8,128)(2,1)S(1)}, u32[]{:S(2)}, u32[]{:S(2)}) %collective-permute-start) | collective-permute-done | bytes 524320 | tf_op jit(solution)/shard_map/ppermute | solution.py:224
  16.3 2.3 %collective-permute-start.8 = (bf16[256,1024]{1,0:T(8,128)(2,1)S(1)}, bf16[256,1024]{1,0:T(8,128)(2,1)S(1)}, u32[]{:S(2)}, u32[]{:S(2)}) collective-permute-start(bf16[256,1024]{1,0:T(8,128)(2,1)S(1)} %slice_select_fusion), channel_id=1, source_target_pairs={{0,4},{1,5},{2,6},{3,7},{4,0},{5,1},{6,2},{7,3},{8,12},{9,13},{10,... | collective-permute-start | bytes 1572872 | tf_op jit(solution)/shard_map/ppermute | solution.py:228
  18.6 1.3 collective-permute-start.1
  19.9 3.6 %collective-permute-start.4 = (bf16[256,1024]{1,0:T(8,128)(2,1)S(1)}, bf16[256,1024]{1,0:T(8,128)(2,1)S(1)}, u32[]{:S(2)}, u32[]{:S(2)}) collective-permute-start(bf16[256,1024]{1,0:T(8,128)(2,1)S(1)} %collective-permute-done), channel_id=1, source_target_pairs={{0,1},{9,8},{1,2},{10,9},{2,3},{11,10},{3,4},{12,11},{4,5},{13,12}... | collective-permute-start | bytes 1572872 | tf_op jit(solution)/shard_map/ppermute | solution.py:233
  23.5 1.5 slice.21
  26.6 2.4 %convolution_convert_fusion.refs_14_ = bf16[1024,1024]{1,0:T(8,128)(2,1)S(1)} fusion(bf16[1024,1024]{1,0:T(8,128)(2,1)S(1)} %copy-done.4, bf16[1024,1024]{1,0:T(8,128)(2,1)S(1)} %bitcast.59), kind=kOutput, calls=%fused_computation.2 | convolution fusion | flops 2148532224 | bytes 6291456 | tf_op jit(solution)/shard_map/dot_general | solution.py:214
  29.0 2.4 %multiply_convert_fusion.refs_1_ = bf16[1024,1024]{1,0:T(8,128)(2,1)S(1)} fusion(bf16[1024,1024]{1,0:T(8,128)(2,1)S(1)} %copy-done.5, bf16[1024,1024]{1,0:T(8,128)(2,1)S(1)} %bitcast.60), kind=kOutput, calls=%fused_computation | convolution fusion | flops 2149580800 | bytes 6291456 | tf_op jit(solution)/shard_map/dot_general | solution.py:214
  31.4 1.7 collective-permute-start.2
  33.1 2.3 %convolution_convert_fusion.1.refs_2_ = bf16[1024,1024]{1,0:T(8,128)(2,1)S(1)} fusion(bf16[1024,1024]{1,0:T(8,128)(2,1)S(1)} %bitcast.61, bf16[1024,1024]{1,0:T(8,128)(2,1)S(1)} %copy-done.3), kind=kOutput, calls=%fused_computation.3 | convolution fusion | flops 2148532224 | bytes 6291456 | tf_op jit(solution)/shard_map/dot_general | solution.py:210
  36.2 16.4 %collective-permute-done.8 = bf16[256,1024]{1,0:T(8,128)(2,1)S(1)} collective-permute-done((bf16[256,1024]{1,0:T(8,128)(2,1)S(1)}, bf16[256,1024]{1,0:T(8,128)(2,1)S(1)}, u32[]{:S(2)}, u32[]{:S(2)}) %collective-permute-start.8) | collective-permute-done | bytes 524320 | tf_op jit(solution)/shard_map/ppermute | solution.py:228
  55.2 24.1 %collective-permute-done.9 = bf16[256,1024]{1,0:T(8,128)(2,1)S(1)} collective-permute-done((bf16[256,1024]{1,0:T(8,128)(2,1)S(1)}, bf16[256,1024]{1,0:T(8,128)(2,1)S(1)}, u32[]{:S(2)}, u32[]{:S(2)}) %collective-permute-start.9) | collective-permute-done | bytes 524320 | tf_op jit(solution)/shard_map/ppermute | solution.py:224
  79.3 1.3 convolution_convert_fusion.9.refs_22_
  83.6 1.8 convolution_convert_fusion.3.refs_15_
  85.4 2.0 convolution_convert_fusion.5.refs_3_
  87.5 2.1 %collective-permute-start.3 = (bf16[768,1024]{1,0:T(8,128)(2,1)S(1)}, bf16[768,1024]{1,0:T(8,128)(2,1)S(1)}, u32[]{:S(2)}, u32[]{:S(2)}) collective-permute-start(bf16[768,1024]{1,0:T(8,128)(2,1)S(1)} %collective-permute-done.2), channel_id=1, source_target_pairs={{0,1},{9,8},{1,2},{10,9},{2,3},{11,10},{3,4},{12,11},{4,5},{13,12}... | collective-permute-start | bytes 4718600 | tf_op jit(solution)/shard_map/ppermute | solution.py:233
  89.6 1.5 collective-permute-start.11
  91.6 1.5 collective-permute-start.5
  93.1 2.9 %collective-permute-done.6 = bf16[256,1024]{1,0:T(8,128)(2,1)S(1)} collective-permute-done((bf16[256,1024]{1,0:T(8,128)(2,1)S(1)}, bf16[256,1024]{1,0:T(8,128)(2,1)S(1)}, u32[]{:S(2)}, u32[]{:S(2)}) %collective-permute-start.6) | collective-permute-done | bytes 524320 | tf_op jit(solution)/shard_map/ppermute | solution.py:224
  96.9 21.3 %collective-permute-done.11 = bf16[256,1024]{1,0:T(8,128)(2,1)S(1)} collective-permute-done((bf16[256,1024]{1,0:T(8,128)(2,1)S(1)}, bf16[256,1024]{1,0:T(8,128)(2,1)S(1)}, u32[]{:S(2)}, u32[]{:S(2)}) %collective-permute-start.11) | collective-permute-done | bytes 524320 | tf_op jit(solution)/shard_map/ppermute | solution.py:228
  118.2 1.3 convolution_convert_fusion.11.refs_20_
  120.8 1.3 convolution_convert_fusion.8.refs_23_
  123.4 1.3 convolution_convert_fusion.12.refs_19_
  125.9 4.3 %collective-permute-done.12 = bf16[256,1024]{1,0:T(8,128)(2,1)S(1)} collective-permute-done((bf16[256,1024]{1,0:T(8,128)(2,1)S(1)}, bf16[256,1024]{1,0:T(8,128)(2,1)S(1)}, u32[]{:S(2)}, u32[]{:S(2)}) %collective-permute-start.12) | collective-permute-done | bytes 524320 | tf_op jit(solution)/shard_map/ppermute | solution.py:224
  130.3 2.3 %collective-permute-start.13 = (bf16[512,1024]{1,0:T(8,128)(2,1)S(1)}, bf16[512,1024]{1,0:T(8,128)(2,1)S(1)}, u32[]{:S(2)}, u32[]{:S(2)}) collective-permute-start(bf16[512,1024]{1,0:T(8,128)(2,1)S(1)} %constant_dynamic-update-slice_fusion.4), channel_id=1, source_target_pairs={{0,1},{1,0},{2,3},{3,2},{4,5},{5,4},{6,7},{7,6},{8,9},{9,8},{10,11... | collective-permute-start | bytes 3145736 | tf_op jit(solution)/shard_map/ppermute | solution.py:225
  135.2 1.3 convolution_convert_fusion.10.refs_21_
  137.8 2.0 convolution_convert_fusion.2.refs_17_
  139.8 1.8 convolution_convert_fusion.4.refs_5_
  141.6 1.3 convolution_convert_fusion.6.refs_25_
  144.2 61.5 %attend.1 = bf16[1024,1024]{1,0:T(8,128)(2,1)S(1)} custom-call(s32[8,16]{1,0:T(8,128)S(1)} %fusion.10.refs_0_, bf16[1024,1024]{1,0:T(8,128)(2,1)S(1)} %multiply_convert_fusion.refs_1_, bf16[1024,1024]{1,0:T(8,128)(2,1)S(1)} %convolution_convert_fusion.1.refs_2_, bf16[768,1024]{1,0:T(8,128)(2,1)S(1)} %convolution_convert_fusion.5.refs_3_, ...), custom_call_target="tpu_custom_call" | custom-call | flops 51539607552 | bytes 37748736 | tf_op jit(solution)/shard_map/attend/pallas_call | solution.py:194
  205.7 3.7 %convert_bitcast_fusion = bf16[1,1024,1024]{2,1,0:T(8,128)(2,1)} fusion(bf16[1024,1024]{1,0:T(8,128)(2,1)S(1)} %attend.1, bf16[1024,1024]{1,0:T(8,128)(2,1)S(1)} %copy-done), kind=kOutput, calls=%fused_computation.1 | convolution fusion | flops 2148532224 | bytes 6291456 | tf_op jit(solution)/shard_map/dot_general | solution.py:311
  (49 shorter events, 20.8 us)
Async XLA Ops:
  0.0 205.7 %copy-start = (bf16[1024,1024]{1,0:T(8,128)(2,1)S(1)}, bf16[1024,1024]{1,0:T(8,128)(2,1)}, u32[]{:S(2)}) copy-start(bf16[1024,1024]{1,0:T(8,128)(2,1)} %param.6) | copy-start | bytes 6291460
  1.2 13.8 %collective-permute-start = (bf16[256,1024]{1,0:T(8,128)(2,1)S(1)}, bf16[256,1024]{1,0:T(8,128)(2,1)S(1)}, u32[]{:S(2)}, u32[]{:S(2)}) collective-permute-start(bf16[256,1024]{1,0:T(8,128)(2,1)S(1)} %slice_bitcast_fusion), channel_id=1, source_target_pairs={{0,8},{8,0},{1,9},{9,1},{2,10},{10,2},{3,11},{11,3},{4,12},{12,4},... | collective-permute-start | bytes 1572872 | tf_op jit(solution)/shard_map/ppermute | solution.py:224
  3.4 8.6 %copy-start.2 = (s32[16,16]{1,0:T(8,128)S(1)}, s32[16,16]{1,0:T(8,128)}, u32[]{:S(2)}) copy-start(s32[16,16]{1,0:T(8,128)} %param.7) | copy-start | bytes 3076
  15.0 10.0 %copy-start.4 = (bf16[1024,1024]{1,0:T(8,128)(2,1)S(1)}, bf16[1024,1024]{1,0:T(8,128)(2,1)}, u32[]{:S(2)}) copy-start(bf16[1024,1024]{1,0:T(8,128)(2,1)} %get-tuple-element.26) | copy-start | bytes 6291460
  16.3 36.3 %collective-permute-start.8 = (bf16[256,1024]{1,0:T(8,128)(2,1)S(1)}, bf16[256,1024]{1,0:T(8,128)(2,1)S(1)}, u32[]{:S(2)}, u32[]{:S(2)}) collective-permute-start(bf16[256,1024]{1,0:T(8,128)(2,1)S(1)} %slice_select_fusion), channel_id=1, source_target_pairs={{0,4},{1,5},{2,6},{3,7},{4,0},{5,1},{6,2},{7,3},{8,12},{9,13},{10,... | collective-permute-start | bytes 1572872 | tf_op jit(solution)/shard_map/ppermute | solution.py:228
  18.6 63.8 %collective-permute-start.1 = (bf16[256,1024]{1,0:T(8,128)(2,1)S(1)}, bf16[256,1024]{1,0:T(8,128)(2,1)S(1)}, u32[]{:S(2)}, u32[]{:S(2)}) collective-permute-start(bf16[256,1024]{1,0:T(8,128)(2,1)S(1)} %slice_select_fusion), channel_id=1, source_target_pairs={{0,2},{1,3},{2,4},{3,5},{4,6},{5,7},{6,0},{7,1},{8,10},{9,11},{10,... | collective-permute-start | bytes 1572872 | tf_op jit(solution)/shard_map/ppermute | solution.py:228
  19.9 33.8 %collective-permute-start.4 = (bf16[256,1024]{1,0:T(8,128)(2,1)S(1)}, bf16[256,1024]{1,0:T(8,128)(2,1)S(1)}, u32[]{:S(2)}, u32[]{:S(2)}) collective-permute-start(bf16[256,1024]{1,0:T(8,128)(2,1)S(1)} %collective-permute-done), channel_id=1, source_target_pairs={{0,1},{9,8},{1,2},{10,9},{2,3},{11,10},{3,4},{12,11},{4,5},{13,12}... | collective-permute-start | bytes 1572872 | tf_op jit(solution)/shard_map/ppermute | solution.py:233
  25.0 1.6 copy-start.1
  26.6 2.4 %copy-start.5 = (bf16[1024,1024]{1,0:T(8,128)(2,1)S(1)}, bf16[1024,1024]{1,0:T(8,128)(2,1)}, u32[]{:S(2)}) copy-start(bf16[1024,1024]{1,0:T(8,128)(2,1)} %get-tuple-element.19) | copy-start | bytes 6291460
  29.0 4.1 %copy-start.3 = (bf16[1024,1024]{1,0:T(8,128)(2,1)S(1)}, bf16[1024,1024]{1,0:T(8,128)(2,1)}, u32[]{:S(2)}) copy-start(bf16[1024,1024]{1,0:T(8,128)(2,1)} %get-tuple-element.21) | copy-start | bytes 6291460
  31.4 50.9 %collective-permute-start.2 = (bf16[768,1024]{1,0:T(8,128)(2,1)S(1)}, bf16[768,1024]{1,0:T(8,128)(2,1)S(1)}, u32[]{:S(2)}, u32[]{:S(2)}) collective-permute-start(bf16[768,1024]{1,0:T(8,128)(2,1)S(1)} %slice.21), channel_id=1, source_target_pairs={{0,8},{8,0},{1,9},{9,1},{2,10},{10,2},{3,11},{11,3},{4,12},{12,4},... | collective-permute-start | bytes 4718600 | tf_op jit(solution)/shard_map/ppermute | solution.py:224
  52.6 26.6 %collective-permute-start.9 = (bf16[256,1024]{1,0:T(8,128)(2,1)S(1)}, bf16[256,1024]{1,0:T(8,128)(2,1)S(1)}, u32[]{:S(2)}, u32[]{:S(2)}) collective-permute-start(bf16[256,1024]{1,0:T(8,128)(2,1)S(1)} %collective-permute-done.8), channel_id=1, source_target_pairs={{0,8},{8,0},{1,9},{9,1},{2,10},{10,2},{3,11},{11,3},{4,12},{12,4},... | collective-permute-start | bytes 1572872 | tf_op jit(solution)/shard_map/ppermute | solution.py:224
  80.5 40.2 %collective-permute-start.10 = (bf16[512,1024]{1,0:T(8,128)(2,1)S(1)}, bf16[512,1024]{1,0:T(8,128)(2,1)S(1)}, u32[]{:S(2)}, u32[]{:S(2)}) collective-permute-start(bf16[512,1024]{1,0:T(8,128)(2,1)S(1)} %constant_dynamic-update-slice_fusion.2), channel_id=1, source_target_pairs={{0,1},{1,0},{2,3},{3,2},{4,5},{5,4},{6,7},{7,6},{8,9},{9,8},{10,11... | collective-permute-start | bytes 3145736 | tf_op jit(solution)/shard_map/ppermute | solution.py:225
  82.4 13.6 %collective-permute-start.6 = (bf16[256,1024]{1,0:T(8,128)(2,1)S(1)}, bf16[256,1024]{1,0:T(8,128)(2,1)S(1)}, u32[]{:S(2)}, u32[]{:S(2)}) collective-permute-start(bf16[256,1024]{1,0:T(8,128)(2,1)S(1)} %collective-permute-done.1), channel_id=1, source_target_pairs={{0,8},{8,0},{1,9},{9,1},{2,10},{10,2},{3,11},{11,3},{4,12},{12,4},... | collective-permute-start | bytes 1572872 | tf_op jit(solution)/shard_map/ppermute | solution.py:224
  87.5 50.3 %collective-permute-start.3 = (bf16[768,1024]{1,0:T(8,128)(2,1)S(1)}, bf16[768,1024]{1,0:T(8,128)(2,1)S(1)}, u32[]{:S(2)}, u32[]{:S(2)}) collective-permute-start(bf16[768,1024]{1,0:T(8,128)(2,1)S(1)} %collective-permute-done.2), channel_id=1, source_target_pairs={{0,1},{9,8},{1,2},{10,9},{2,3},{11,10},{3,4},{12,11},{4,5},{13,12}... | collective-permute-start | bytes 4718600 | tf_op jit(solution)/shard_map/ppermute | solution.py:233
  89.6 28.6 %collective-permute-start.11 = (bf16[256,1024]{1,0:T(8,128)(2,1)S(1)}, bf16[256,1024]{1,0:T(8,128)(2,1)S(1)}, u32[]{:S(2)}, u32[]{:S(2)}) collective-permute-start(bf16[256,1024]{1,0:T(8,128)(2,1)S(1)} %slice_select_fusion), channel_id=1, source_target_pairs={{0,6},{1,7},{2,0},{3,1},{4,2},{5,3},{6,4},{7,5},{8,14},{9,15},{10,... | collective-permute-start | bytes 1572872 | tf_op jit(solution)/shard_map/ppermute | solution.py:228
  91.6 31.7 %collective-permute-start.5 = (bf16[512,1024]{1,0:T(8,128)(2,1)S(1)}, bf16[512,1024]{1,0:T(8,128)(2,1)S(1)}, u32[]{:S(2)}, u32[]{:S(2)}) collective-permute-start(bf16[512,1024]{1,0:T(8,128)(2,1)S(1)} %maximum_select_fusion), channel_id=1, source_target_pairs={{0,1},{1,0},{2,3},{3,2},{4,5},{5,4},{6,7},{7,6},{8,9},{9,8},{10,11... | collective-permute-start | bytes 3145736 | tf_op jit(solution)/shard_map/ppermute | solution.py:225
  96.0 39.2 %collective-permute-start.7 = (bf16[512,1024]{1,0:T(8,128)(2,1)S(1)}, bf16[512,1024]{1,0:T(8,128)(2,1)S(1)}, u32[]{:S(2)}, u32[]{:S(2)}) collective-permute-start(bf16[512,1024]{1,0:T(8,128)(2,1)S(1)} %constant_dynamic-update-slice_fusion), channel_id=1, source_target_pairs={{0,1},{1,0},{2,3},{3,2},{4,5},{5,4},{6,7},{7,6},{8,9},{9,8},{10,11... | collective-permute-start | bytes 3145736 | tf_op jit(solution)/shard_map/ppermute | solution.py:225
  118.2 12.1 %collective-permute-start.12 = (bf16[256,1024]{1,0:T(8,128)(2,1)S(1)}, bf16[256,1024]{1,0:T(8,128)(2,1)S(1)}, u32[]{:S(2)}, u32[]{:S(2)}) collective-permute-start(bf16[256,1024]{1,0:T(8,128)(2,1)S(1)} %collective-permute-done.11), channel_id=1, source_target_pairs={{0,8},{8,0},{1,9},{9,1},{2,10},{10,2},{3,11},{11,3},{4,12},{12,4},... | collective-permute-start | bytes 1572872 | tf_op jit(solution)/shard_map/ppermute | solution.py:224
  130.3 11.3 %collective-permute-start.13 = (bf16[512,1024]{1,0:T(8,128)(2,1)S(1)}, bf16[512,1024]{1,0:T(8,128)(2,1)S(1)}, u32[]{:S(2)}, u32[]{:S(2)}) collective-permute-start(bf16[512,1024]{1,0:T(8,128)(2,1)S(1)} %constant_dynamic-update-slice_fusion.4), channel_id=1, source_target_pairs={{0,1},{1,0},{2,3},{3,2},{4,5},{5,4},{6,7},{7,6},{8,9},{9,8},{10,11... | collective-permute-start | bytes 3145736 | tf_op jit(solution)/shard_map/ppermute | solution.py:225

commit v3 on v1

--- a/solution.py
+++ b/solution.py
@@ -121,6 +121,23 @@
             row_out_ref[0, 1:2, at(index, 2 * BLK)] = count_all
         return count_all
 
+    def whole_row(index):
+        query = queries(index)
+        shift = jnp.full((1, 2 * BLK), -jnp.inf, f32) if first else row_in_ref[0, 0:1, at(index, 2 * BLK)]
+        old = shift
+
+        def largest(n, shift):
+            return jnp.maximum(shift, jnp.max(score(index, chunk * n, query), axis=0, keepdims=True))
+
+        shift = lax.fori_loop(0, count // chunk, largest, shift)
+
+        def add(n, total):
+            raised = jnp.exp(score(index, chunk * n, query) - shift).astype(bf16)
+            return total + gather(values(index, chunk * n), raised)
+
+        total = lax.fori_loop(0, count // chunk, add, jnp.zeros((LANES + 16, 2 * BLK), f32))
+        finish(index, shift, total, None if first else jnp.exp(old - shift))
+
     def one(index):
         query = queries(index)
         total = None
@@ -132,23 +149,6 @@
             part = gather(values(index, which), jnp.exp(scores - shift).astype(bf16))
             total = part if total is None else total + part
         return finish(index, shift, total)
-
-    def whole_row(index):
-        query = queries(index)
-        shift = jnp.full((1, 2 * BLK), -jnp.inf, f32) if first else row_in_ref[0, 0:1, at(index, 2 * BLK)]
-        old = shift
-
-        def largest(n, shift):
-            return jnp.maximum(shift, jnp.max(score(index, chunk * n, query), axis=0, keepdims=True))
-
-        shift = lax.fori_loop(0, count // chunk, largest, shift)
-
-        def add(n, total):
-            raised = jnp.exp(score(index, chunk * n, query) - shift).astype(bf16)
-            return total + gather(values(index, chunk * n), raised)
-
-        total = lax.fori_loop(0, count // chunk, add, jnp.zeros((LANES + 16, 2 * BLK), f32))
-        finish(index, shift, total, None if first else jnp.exp(old - shift))
 
     def body(number, peak):
         for n in range(together):
@@ -218,9 +218,6 @@
     swap = lambda rows: lax.ppermute(rows, "head", [(0, 1), (1, 0)])
     beside = lambda rows: lax.ppermute(rows, "blk", [(s, s ^ 1) for s in range(strides)])
 
-    def along(rows, k):
-        return lax.ppermute(rows, "blk", [(s, (s + 2 * k) % strides) for s in range(strides)])
-
     steps = []
     for s in range(strides - 1):
         steps += [(s, s + 1), (strides + s + 1, strides + s)]
@@ -230,16 +227,16 @@
     other_end, own, weights = lax.optimization_barrier((other_end, own, weights))
     carried = jnp.where(low, other_end, own[cut : cut + half])
     other = swap(own[:-half])
-    slots = [None] * chips
-    slots[2:-1] = [along(carried, k) for k in range(2, chips - 1)]
-    slots[1] = along(carried, 1)
-    slots[1], after = lax.optimization_barrier((slots[1], carried))
-    slots[-1] = along(after, chips - 1)
-    slots[0] = jnp.concatenate([carried, jnp.where(low, other[-half:], own[-half:])], axis=0)
-    slots[1:] = [jnp.concatenate([rows, swap(rows)], axis=0) for rows in slots[1:]]
-    pieces = [own, other, other_end, to_next(other), to_next(other_end), beside(slots[0])]
-    for rows in slots[1:]:
-        pieces += [rows, beside(rows)]
+    parities = [[s for s in range(strides) if s % 2 == core] for core in range(2)]
+    column = lax.all_gather(carried, "blk", axis=0, tiled=True, axis_index_groups=parities)
+    turned_column = jnp.concatenate([column, column], axis=0)
+    foreign = lax.dynamic_slice_in_dim(turned_column, (stride // 2 + 1) * half, column.shape[0] - half, 0)
+    across = swap(foreign)
+    nearby = jnp.where(low, jnp.concatenate([other_end, other[-half:]], axis=0), own[cut:])
+    pieces = [own, other, other_end, to_next(other), to_next(other_end), beside(nearby)]
+    pieces += [foreign, across, beside(foreign), beside(across)]
+    base = 28
+    span = 2 * (chips - 1)
 
     def position(block):
         of, inside = block // SB, block % SB
@@ -247,9 +244,10 @@
         mine = inside % 8 + jnp.where(inside // 8 == place, 0, 8)
         edge = jnp.where(rel < 0, rel + SB + 8, rel)
         order = inside - (SB - SUMB)
-        k = (stride // 2 - of // 2) % chips
+        k = (of // 2 - stride // 2) % chips
         turned = (order // 2 ^ (1 - place)) * 2 + order % 2
-        far = jnp.where(k == 0, 24, 28 + (k - 1) * 8 + jnp.where(of % 2 == stride % 2, 0, 4)) + turned
+        part = jnp.where(of % 2 == stride % 2, 0, 2) + jnp.where(order // 2 == 1 - place, 0, 1)
+        far = jnp.where(k == 0, 24 + turned, base + part * span + (k - 1) * 2 + order % 2)
         return jnp.where(of == stride, mine, edge), jnp.where(of == stride, mine, far)
 
     return pieces, weights, position
@@ -301,7 +299,7 @@
     query = project_columns(query_weight, own, HD**-0.5)
     keys = [project_rows(rows, key_weight) for rows in pieces]
     values = [project_columns(value_weight, rows) for rows in pieces]
-    mixed = attend("attend", table, query, keys, values, [], True, 2, 8)
+    mixed = attend("attend", table, query, keys, values, [], True, 2, 4)
     out = jnp.dot(mixed, out_weight, preferred_element_type=jnp.float32).astype(jnp.bfloat16)
     return out.reshape(tokens.shape)
 

time: 227 us -> 214 us (0.943)
  waiting for transfers between devices: 84.7 us -> 50.9 us
  matrix products: 40.6 us -> 59.9 us
  between operations: 0.35 us -> 13.8 us
  starting transfers between devices: 24 us -> 10.9 us
  Pallas kernels: 72 us -> 66.2 us
  other arithmetic: 0.28 us -> 4.16 us
    ppermute x3 -> x0, waiting for transfers between devices: 31.2 us -> none  [along(): lax.ppermute(rows, 'blk', [(s, (s + 2 * k) % strides) for s in range(stri...]
    dot_general x13 -> x11, matrix products: 20.7 us -> 31.5 us  [project_columns(): lax.dot_general(weight, rows, (((1,), (1,)), ((), ())), preferred_element...]
    ppermute x5 -> x3, starting transfers between devices: 11.2 us -> 1.42 us  [rows_by_axes(): swap = lambda rows: lax.ppermute(rows, 'head', [(0, 1), (1, 0)])]
    dot_general x12 -> x10, matrix products: 16.2 us -> 24.7 us  [project_rows(): jnp.dot(rows, weight, preferred_element_type=jnp.float32)]
    pallas_call x1, Pallas kernels: 63.4 us -> 57.6 us  [attend(): pl.pallas_call(functools.partial(attend_kernel, not state, last, blocks,...]
    ppermute x4 -> x3, starting transfers between devices: 4.18 us -> 1.41 us  [rows_by_axes(): lax.ppermute(rows, 'blk', [(s, s ^ 1) for s in range(strides)])]
    concatenate x1, other arithmetic: 0.07 us -> 2.81 us  [rows_by_axes(): turned_column = jnp.concatenate([column, column], axis=0)]
    ppermute x5 -> x3, waiting for transfers between devices: 53.5 us -> 50.8 us  [rows_by_axes(): swap = lambda rows: lax.ppermute(rows, 'head', [(0, 1), (1, 0)])]
  transfers between devices with their start and end apart: 14 -> 9, of which waited for: 6 -> 3; matrix products, arithmetic and copies ran while one was open for 15% -> 28% of each run, Pallas kernels for 4% -> 4%
where the time goes in v3:
time: 214 us; the launch traced here: 212 us
  Pallas kernels  66.2 us (31%)
  matrix products  59.9 us (28%)
  waiting for transfers between devices  50.9 us (24%)
  between operations  13.8 us (6%)
  starting transfers between devices  10.9 us (5%)
  local copies, waits for them, and re-layouts  6.08 us (3%)
  other arithmetic  4.16 us (2%)
    pallas_call x1, Pallas kernels, attend(): pl.pallas_call(functools.partial(attend_kernel, not state, last, blocks,...  57.6 us
    ppermute x3, waiting for transfers between devices, rows_by_axes(): swap = lambda rows: lax.ppermute(rows, 'head', [(0, 1), (1, 0)])  50.8 us
    dot_general x11, matrix products, project_columns(): lax.dot_general(weight, rows, (((1,), (1,)), ((), ())), preferred_element...  31.5 us
    dot_general x10, matrix products, project_rows(): jnp.dot(rows, weight, preferred_element_type=jnp.float32)  24.7 us
    pallas_call x1, Pallas kernels, split_weights(): pl.pallas_call(split_kernel, grid=(PAIRS,), in_specs=[pl.BlockSpec((D, 3...  8.61 us
    ppermute x2, starting transfers between devices, rows_by_axes(): to_next = lambda rows: lax.ppermute(rows, ('head', 'blk'), steps)  8.1 us
  transfers between devices with their start and end apart: 9, of which 3 were waited for; matrix products, arithmetic and copies ran while one was open for 28% of the time, Pallas kernels for 4%

profile of v3, /device:TPU:11, one launch (start us, length us, event | category | flops | bytes accessed | tf_op | source)
XLA Modules:
  0.0 211.9 jit_solution(14033356241555744880)
XLA Ops:
  7.8 1.3 collective-permute-start
  9.1 8.6 %split_weights.1 = (bf16[1024,1024]{1,0:T(8,128)(2,1)}, bf16[1024,1024]{1,0:T(8,128)(2,1)}, bf16[1024,1024]{1,0:T(8,128)(2,1)}) custom-call(bf16[1024,3072]{1,0:T(8,128)(2,1)} %weight_ref.1), custom_call_target="tpu_custom_call" | custom-call | bytes 12582912 | tf_op jit(solution)/shard_map/split_weights/pallas_call | solution.py:41
  17.8 2.9 %collective-permute-done = bf16[256,1024]{1,0:T(8,128)(2,1)S(1)} collective-permute-done((bf16[256,1024]{1,0:T(8,128)(2,1)S(1)}, bf16[256,1024]{1,0:T(8,128)(2,1)S(1)}, u32[]{:S(2)}, u32[]{:S(2)}) %collective-permute-start) | collective-permute-done | bytes 524320 | tf_op jit(solution)/shard_map/ppermute | solution.py:218
  20.6 4.6 %collective-permute-start.3 = (bf16[256,1024]{1,0:T(8,128)(2,1)S(1)}, bf16[256,1024]{1,0:T(8,128)(2,1)}, u32[]{:S(2)}, u32[]{:S(2)}) collective-permute-start(bf16[256,1024]{1,0:T(8,128)(2,1)S(1)} %collective-permute-done), channel_id=1, source_target_pairs={{0,1},{9,8},{1,2},{10,9},{2,3},{11,10},{3,4},{12,11},{4,5},{13,12}... | collective-permute-start | bytes 1572872 | tf_op jit(solution)/shard_map/ppermute | solution.py:224
  25.3 2.3 %convolution_convert_fusion.19.refs_4_ = bf16[256,1024]{1,0:T(8,128)(2,1)S(1)} fusion(bf16[256,1024]{1,0:T(8,128)(2,1)S(1)} %collective-permute-done, bf16[1024,1024]{1,0:T(8,128)(2,1)} %get-tuple-element.18), kind=kOutput, calls=%fused_computation.24 | convolution fusion | flops 537133056 | bytes 3145728 | tf_op jit(solution)/shard_map/dot_general | solution.py:204
  29.7 3.7 %convolution_convert_fusion.1.refs_2_ = bf16[1024,1024]{1,0:T(8,128)(2,1)} fusion(bf16[1024,1024]{1,0:T(8,128)(2,1)S(1)} %bitcast.51, bf16[1024,1024]{1,0:T(8,128)(2,1)S(1)} %copy-done.13), kind=kOutput, calls=%fused_computation.5 | convolution fusion | flops 2148532224 | bytes 6291456 | tf_op jit(solution)/shard_map/dot_general | solution.py:204
  33.4 1.6 convolution_convert_fusion.17.refs_14_
  36.0 6.1 %convolution_convert_fusion.refs_12_ = bf16[1024,1024]{1,0:T(8,128)(2,1)} fusion(bf16[1024,1024]{1,0:T(8,128)(2,1)} %get-tuple-element.20, bf16[1024,1024]{1,0:T(8,128)(2,1)} %bitcast.49), kind=kOutput, calls=%fused_computation.4 | convolution fusion | flops 2148532224 | bytes 6291456 | tf_op jit(solution)/shard_map/dot_general | solution.py:208
  42.1 3.7 %multiply_convert_fusion.refs_1_ = bf16[1024,1024]{1,0:T(8,128)(2,1)} fusion(bf16[1024,1024]{1,0:T(8,128)(2,1)S(1)} %copy-done.19, bf16[1024,1024]{1,0:T(8,128)(2,1)S(1)} %bitcast.53), kind=kOutput, calls=%fused_computation.2 | convolution fusion | flops 2149580800 | bytes 6291456 | tf_op jit(solution)/shard_map/dot_general | solution.py:208
  45.8 2.6 %convolution_convert_fusion.16.refs_16_ = bf16[1024,256]{1,0:T(8,128)(2,1)} fusion(bf16[1024,1024]{1,0:T(8,128)(2,1)S(1)} %copy-done.17, bf16[256,1024]{1,0:T(8,128)(2,1)} %collective-permute-done.3), kind=kOutput, calls=%fused_computation.21 | convolution fusion | flops 537133056 | bytes 3145728 | tf_op jit(solution)/shard_map/dot_general | solution.py:208
  48.4 22.6 %collective-permute-done.1 = bf16[768,1024]{1,0:T(8,128)(2,1)} collective-permute-done((bf16[768,1024]{1,0:T(8,128)(2,1)}, bf16[768,1024]{1,0:T(8,128)(2,1)}, u32[]{:S(2)}, u32[]{:S(2)}) %collective-permute-start.1) | collective-permute-done | bytes 1572896 | tf_op jit(solution)/shard_map/ppermute | solution.py:218
  72.6 1.8 convolution_convert_fusion.18.refs_6_
  74.4 3.5 %collective-permute-start.2 = (bf16[768,1024]{1,0:T(8,128)(2,1)}, bf16[768,1024]{1,0:T(8,128)(2,1)}, u32[]{:S(2)}, u32[]{:S(2)}) collective-permute-start(bf16[768,1024]{1,0:T(8,128)(2,1)} %collective-permute-done.1), channel_id=1, source_target_pairs={{0,1},{9,8},{1,2},{10,9},{2,3},{11,10},{3,4},{12,11},{4,5},{13,12}... | collective-permute-start | bytes 4718600 | tf_op jit(solution)/shard_map/ppermute | solution.py:224
  77.9 4.4 %convolution_convert_fusion.7.refs_13_ = bf16[1024,768]{1,0:T(8,128)(2,1)} fusion(bf16[1024,1024]{1,0:T(8,128)(2,1)S(1)} %copy-done.17, bf16[768,1024]{1,0:T(8,128)(2,1)} %collective-permute-done.1), kind=kOutput, calls=%fused_computation.11 | convolution fusion | flops 1611399168 | bytes 5242880 | tf_op jit(solution)/shard_map/dot_general | solution.py:208
  82.3 4.4 %convolution_convert_fusion.13.refs_3_ = bf16[768,1024]{1,0:T(8,128)(2,1)} fusion(bf16[768,1024]{1,0:T(8,128)(2,1)} %collective-permute-done.1, bf16[1024,1024]{1,0:T(8,128)(2,1)S(1)} %copy-done.14), kind=kOutput, calls=%fused_computation.17 | convolution fusion | flops 1611399168 | bytes 5242880 | tf_op jit(solution)/shard_map/dot_general | solution.py:204
  86.6 2.3 %convolution_convert_fusion.14.refs_17_ = bf16[1024,512]{1,0:T(8,128)(2,1)} fusion(bf16[1024,1024]{1,0:T(8,128)(2,1)S(1)} %copy-done.17, bf16[512,1024]{1,0:T(8,128)(2,1)S(1)} %collective-permute-done.4), kind=kOutput, calls=%fused_computation.19 | convolution fusion | flops 1074266112 | bytes 4194304 | tf_op jit(solution)/shard_map/dot_general | solution.py:208
  88.9 2.2 %convolution_convert_fusion.15.refs_7_ = bf16[512,1024]{1,0:T(8,128)(2,1)} fusion(bf16[512,1024]{1,0:T(8,128)(2,1)S(1)} %collective-permute-done.4, bf16[1024,1024]{1,0:T(8,128)(2,1)S(1)} %copy-done.14), kind=kOutput, calls=%fused_computation.20 | convolution fusion | flops 1074266112 | bytes 4194304 | tf_op jit(solution)/shard_map/dot_general | solution.py:204
  91.1 2.8 %fusion = bf16[768,1024]{1,0:T(8,128)(2,1)S(1)} fusion(s32[]{:T(128)S(6)} %select_n.122, bf16[1024,1024]{1,0:T(8,128)(2,1)} %all-gather.2.cloned.1.call-done), kind=kLoop, calls=%fused_computation.18 | loop fusion | flops 3145728 | bytes 3670020 | tf_op jit(solution)/shard_map/concatenate | solution.py:232
  94.1 1.8 convolution_convert_fusion.11.refs_8_
  95.9 1.8 convolution_convert_fusion.5.refs_18_
  97.8 3.2 %convolution_convert_fusion.6.refs_15_ = bf16[1024,768]{1,0:T(8,128)(2,1)S(1)} fusion(bf16[1024,1024]{1,0:T(8,128)(2,1)S(1)} %copy-done.18, bf16[768,1024]{1,0:T(8,128)(2,1)} %collective-permute-done.2), kind=kOutput, calls=%fused_computation.10 | convolution fusion | flops 1611399168 | bytes 5242880 | tf_op jit(solution)/shard_map/dot_general | solution.py:208
  101.0 3.2 %convolution_convert_fusion.12.refs_5_ = bf16[768,1024]{1,0:T(8,128)(2,1)S(1)} fusion(bf16[768,1024]{1,0:T(8,128)(2,1)} %collective-permute-done.2, bf16[1024,1024]{1,0:T(8,128)(2,1)S(1)} %copy-done.15), kind=kOutput, calls=%fused_computation.16 | convolution fusion | flops 1611399168 | bytes 5242880 | tf_op jit(solution)/shard_map/dot_general | solution.py:204
  104.2 25.4 %collective-permute-done.5 = bf16[768,1024]{1,0:T(8,128)(2,1)S(1)} collective-permute-done((bf16[768,1024]{1,0:T(8,128)(2,1)S(1)}, bf16[768,1024]{1,0:T(8,128)(2,1)S(1)}, u32[]{:S(2)}, u32[]{:S(2)}) %collective-permute-start.5) | collective-permute-done | bytes 1572896 | tf_op jit(solution)/shard_map/ppermute | solution.py:218
  129.6 1.3 collective-permute-start.7
  130.9 2.1 convolution_convert_fusion.3.refs_20_
  133.0 1.8 convolution_convert_fusion.9.refs_10_
  134.8 1.8 convolution_convert_fusion.4.refs_19_
  136.6 1.8 convolution_convert_fusion.10.refs_9_
  138.5 1.8 convolution_convert_fusion.2.refs_21_
  140.4 1.8 convolution_convert_fusion.8.refs_11_
  143.8 57.6 %attend.1 = bf16[1024,1024]{1,0:T(8,128)(2,1)S(1)} custom-call(s32[8,16]{1,0:T(8,128)S(1)} %fusion.7.refs_0_, bf16[1024,1024]{1,0:T(8,128)(2,1)S(1)} %copy-done.9, bf16[1024,1024]{1,0:T(8,128)(2,1)S(1)} %copy-done.6, bf16[768,1024]{1,0:T(8,128)(2,1)S(1)} %copy-done.4, bf16[256,1024]{1,0:T(8,128)(2,1)S(1)} %convolution_convert_fusion.19.refs_4_, ...), custom_call_target="tpu_custom_call" | custom-call | flops 51539607552 | bytes 37748736 | tf_op jit(solution)/shard_map/attend/pallas_call | solution.py:188
  201.4 3.7 %convert_bitcast_fusion = bf16[1,1024,1024]{2,1,0:T(8,128)(2,1)} fusion(bf16[1024,1024]{1,0:T(8,128)(2,1)S(1)} %attend.1, bf16[1024,1024]{1,0:T(8,128)(2,1)S(1)} %copy-done), kind=kOutput, calls=%fused_computation.3 | convolution fusion | flops 2148532224 | bytes 6291456 | tf_op jit(solution)/shard_map/dot_general | solution.py:303
  (59 shorter events, 7.7 us)
Async XLA Ops:
  6.5 194.8 %copy-start = (bf16[1024,1024]{1,0:T(8,128)(2,1)S(1)}, bf16[1024,1024]{1,0:T(8,128)(2,1)}, u32[]{:S(2)}) copy-start(bf16[1024,1024]{1,0:T(8,128)(2,1)} %param.6) | copy-start | bytes 6291460
  6.5 84.6 %all-gather.2.cloned.1.call-start = ((), (), s32[]{:S(2)}) async-start(), calls=%async_computation | async-start | bytes 2621440 | tf_op jit(solution)/shard_map/all_gather | solution.py:231
  7.8 12.9 %collective-permute-start = (bf16[256,1024]{1,0:T(8,128)(2,1)S(1)}, bf16[256,1024]{1,0:T(8,128)(2,1)S(1)}, u32[]{:S(2)}, u32[]{:S(2)}) collective-permute-start(bf16[256,1024]{1,0:T(8,128)(2,1)S(1)} %slice_bitcast_fusion), channel_id=1, source_target_pairs={{0,8},{8,0},{1,9},{9,1},{2,10},{10,2},{3,11},{11,3},{4,12},{12,4},... | collective-permute-start | bytes 1572872 | tf_op jit(solution)/shard_map/ppermute | solution.py:218
  9.1 8.6 %copy-start.12 = (s32[16,16]{1,0:T(8,128)S(1)}, s32[16,16]{1,0:T(8,128)}, u32[]{:S(2)}) copy-start(s32[16,16]{1,0:T(8,128)} %param.7) | copy-start | bytes 3076
  17.7 9.9 %copy-start.10 = (bf16[1,1024,1024]{2,1,0:T(8,128)(2,1)S(1)}, bf16[1,1024,1024]{2,1,0:T(8,128)(2,1)}, u32[]{:S(2)}) copy-start(bf16[1,1024,1024]{2,1,0:T(8,128)(2,1)} %param.4) | copy-start | bytes 6291460
  20.6 25.2 %collective-permute-start.3 = (bf16[256,1024]{1,0:T(8,128)(2,1)S(1)}, bf16[256,1024]{1,0:T(8,128)(2,1)}, u32[]{:S(2)}, u32[]{:S(2)}) collective-permute-start(bf16[256,1024]{1,0:T(8,128)(2,1)S(1)} %collective-permute-done), channel_id=1, source_target_pairs={{0,1},{9,8},{1,2},{10,9},{2,3},{11,10},{3,4},{12,11},{4,5},{13,12}... | collective-permute-start | bytes 1572872 | tf_op jit(solution)/shard_map/ppermute | solution.py:224
  27.6 2.2 %copy-start.13 = (bf16[1024,1024]{1,0:T(8,128)(2,1)S(1)}, bf16[1024,1024]{1,0:T(8,128)(2,1)}, u32[]{:S(2)}) copy-start(bf16[1024,1024]{1,0:T(8,128)(2,1)} %get-tuple-element.18) | copy-start | bytes 6291460
  29.7 3.7 %copy-start.16 = (bf16[1024,1024]{1,0:T(8,128)(2,1)S(1)}, bf16[1024,1024]{1,0:T(8,128)(2,1)}, u32[]{:S(2)}) copy-start(bf16[1024,1024]{1,0:T(8,128)(2,1)} %get-tuple-element.20) | copy-start | bytes 6291460
  35.0 36.0 %collective-permute-start.1 = (bf16[768,1024]{1,0:T(8,128)(2,1)}, bf16[768,1024]{1,0:T(8,128)(2,1)}, u32[]{:S(2)}, u32[]{:S(2)}) collective-permute-start(bf16[768,1024]{1,0:T(8,128)(2,1)} %slice.20), channel_id=1, source_target_pairs={{0,8},{8,0},{1,9},{9,1},{2,10},{10,2},{3,11},{11,3},{4,12},{12,4},... | collective-permute-start | bytes 4718600 | tf_op jit(solution)/shard_map/ppermute | solution.py:218
  36.0 6.2 %copy-start.11 = (bf16[1,1024,1024]{2,1,0:T(8,128)(2,1)S(1)}, bf16[1,1024,1024]{2,1,0:T(8,128)(2,1)}, u32[]{:S(2)}) copy-start(bf16[1,1024,1024]{2,1,0:T(8,128)(2,1)} %param.4) | copy-start | bytes 6291460
  36.0 6.2 %copy-start.19 = (bf16[1024,1024]{1,0:T(8,128)(2,1)S(1)}, bf16[1024,1024]{1,0:T(8,128)(2,1)}, u32[]{:S(2)}) copy-start(bf16[1024,1024]{1,0:T(8,128)(2,1)} %get-tuple-element.16) | copy-start | bytes 6291460
  42.1 3.7 %copy-start.17 = (bf16[1024,1024]{1,0:T(8,128)(2,1)S(1)}, bf16[1024,1024]{1,0:T(8,128)(2,1)}, u32[]{:S(2)}) copy-start(bf16[1024,1024]{1,0:T(8,128)(2,1)} %get-tuple-element.20) | copy-start | bytes 6291460
  48.4 24.2 %copy-start.14 = (bf16[1024,1024]{1,0:T(8,128)(2,1)S(1)}, bf16[1024,1024]{1,0:T(8,128)(2,1)}, u32[]{:S(2)}) copy-start(bf16[1024,1024]{1,0:T(8,128)(2,1)} %get-tuple-element.18) | copy-start | bytes 6291460
  72.5 14.1 %collective-permute-start.4 = (bf16[512,1024]{1,0:T(8,128)(2,1)S(1)}, bf16[512,1024]{1,0:T(8,128)(2,1)S(1)}, u32[]{:S(2)}, u32[]{:S(2)}) collective-permute-start(bf16[512,1024]{1,0:T(8,128)(2,1)S(1)} %maximum_select_fusion), channel_id=1, source_target_pairs={{0,1},{1,0},{2,3},{3,2},{4,5},{5,4},{6,7},{7,6},{8,9},{9,8},{10,11... | collective-permute-start | bytes 3145736 | tf_op jit(solution)/shard_map/ppermute | solution.py:219
  74.4 23.4 %collective-permute-start.2 = (bf16[768,1024]{1,0:T(8,128)(2,1)}, bf16[768,1024]{1,0:T(8,128)(2,1)}, u32[]{:S(2)}, u32[]{:S(2)}) collective-permute-start(bf16[768,1024]{1,0:T(8,128)(2,1)} %collective-permute-done.1), channel_id=1, source_target_pairs={{0,1},{9,8},{1,2},{10,9},{2,3},{11,10},{3,4},{12,11},{4,5},{13,12}... | collective-permute-start | bytes 4718600 | tf_op jit(solution)/shard_map/ppermute | solution.py:224
  91.1 3.0 %copy-start.15 = (bf16[1024,1024]{1,0:T(8,128)(2,1)S(1)}, bf16[1024,1024]{1,0:T(8,128)(2,1)}, u32[]{:S(2)}) copy-start(bf16[1024,1024]{1,0:T(8,128)(2,1)} %get-tuple-element.18) | copy-start | bytes 6291460
  93.9 2.0 copy-start.18
  93.9 37.0 %collective-permute-start.6 = (bf16[768,1024]{1,0:T(8,128)(2,1)S(1)}, bf16[768,1024]{1,0:T(8,128)(2,1)S(1)}, u32[]{:S(2)}, u32[]{:S(2)}) collective-permute-start(bf16[768,1024]{1,0:T(8,128)(2,1)S(1)} %fusion), channel_id=1, source_target_pairs={{0,1},{1,0},{2,3},{3,2},{4,5},{5,4},{6,7},{7,6},{8,9},{9,8},{10,11... | collective-permute-start | bytes 4718600 | tf_op jit(solution)/shard_map/ppermute | solution.py:219
  94.0 35.6 %collective-permute-start.5 = (bf16[768,1024]{1,0:T(8,128)(2,1)S(1)}, bf16[768,1024]{1,0:T(8,128)(2,1)S(1)}, u32[]{:S(2)}, u32[]{:S(2)}) collective-permute-start(bf16[768,1024]{1,0:T(8,128)(2,1)S(1)} %fusion), channel_id=1, source_target_pairs={{0,8},{8,0},{1,9},{9,1},{2,10},{10,2},{3,11},{11,3},{4,12},{12,4},... | collective-permute-start | bytes 4718600 | tf_op jit(solution)/shard_map/ppermute | solution.py:218
  129.6 8.8 %collective-permute-start.7 = (bf16[768,1024]{1,0:T(8,128)(2,1)S(1)}, bf16[768,1024]{1,0:T(8,128)(2,1)S(1)}, u32[]{:S(2)}, u32[]{:S(2)}) collective-permute-start(bf16[768,1024]{1,0:T(8,128)(2,1)S(1)} %collective-permute-done.5), channel_id=1, source_target_pairs={{0,1},{1,0},{2,3},{3,2},{4,5},{5,4},{6,7},{7,6},{8,9},{9,8},{10,11... | collective-permute-start | bytes 4718600 | tf_op jit(solution)/shard_map/ppermute | solution.py:219
  138.4 3.7 %copy-start.8 = (bf16[1024,1024]{1,0:T(8,128)(2,1)S(1)}, bf16[1024,1024]{1,0:T(8,128)(2,1)}, u32[]{:S(2)}) copy-start(bf16[1024,1024]{1,0:T(8,128)(2,1)} %convolution_convert_fusion.refs_12_) | copy-start | bytes 6291460
  138.4 3.7 %copy-start.9 = (bf16[1024,1024]{1,0:T(8,128)(2,1)S(1)}, bf16[1024,1024]{1,0:T(8,128)(2,1)}, u32[]{:S(2)}) copy-start(bf16[1024,1024]{1,0:T(8,128)(2,1)} %multiply_convert_fusion.refs_1_) | copy-start | bytes 6291460
  140.3 1.9 copy-start.1
  140.3 1.9 copy-start.2
  140.3 1.9 copy-start.3
  140.3 2.1 copy-start.4
  140.3 2.4 %copy-start.5 = (bf16[1024,512]{1,0:T(8,128)(2,1)S(1)}, bf16[1024,512]{1,0:T(8,128)(2,1)}, u32[]{:S(2)}) copy-start(bf16[1024,512]{1,0:T(8,128)(2,1)} %convolution_convert_fusion.14.refs_17_) | copy-start | bytes 3145732
  140.3 3.0 %copy-start.6 = (bf16[1024,1024]{1,0:T(8,128)(2,1)S(1)}, bf16[1024,1024]{1,0:T(8,128)(2,1)}, u32[]{:S(2)}) copy-start(bf16[1024,1024]{1,0:T(8,128)(2,1)} %convolution_convert_fusion.1.refs_2_) | copy-start | bytes 6291460
  140.4 3.4 %copy-start.7 = (bf16[1024,768]{1,0:T(8,128)(2,1)S(1)}, bf16[1024,768]{1,0:T(8,128)(2,1)}, u32[]{:S(2)}) copy-start(bf16[1024,768]{1,0:T(8,128)(2,1)} %convolution_convert_fusion.7.refs_13_) | copy-start | bytes 4718596
Sparse Core Ops, SparseCore 0:
  36.1 44.5 all-gather.1
